TPU v7x, 128 devices: a whole 4x4x4 slice. The times are simulated.
128 devices in a mesh: head: 2 (over z_lo), blk: 64 (over y, x, z_hi, core).
Axes of the slice: x: 4, y: 4, z: 4 (z_hi: 2, z_lo: 2; z = z_hi * 2 + z_lo), core: 2. Of those that a mesh axis runs over, the one named last changes fastest.
Arguments:
- tokens: bfloat16 [16384, 2048], P(('head', 'blk')), may hold values from -6 to 6
- norm_gain: float32 [2048], replicated, may hold values from 0.5 to 1.5
- w_query: bfloat16 [2048, 4096], P('blk', 'head'), may hold values from -0.125 to 0.125
- key_weight: bfloat16 [2048, 512], P('blk', 'head'), may hold values from -0.125 to 0.125
- value_weight: bfloat16 [2048, 512], P('blk', 'head'), may hold values from -0.125 to 0.125
- query_gain: float32 [128], replicated, may hold values from 0.25 to 1.75
- key_gain: float32 [128], replicated, may hold values from 0.25 to 1.75
- w_out: bfloat16 [4096, 2048], P('head', 'blk'), may hold values from -0.75 to 0.75
- mix_gain: float32 [2048], replicated, may hold values from 0.5 to 1.5
- w_router: bfloat16 [128, 2048], P('head', 'blk'), may hold values from -0.0625 to 0.0625
- expert_gate_up: bfloat16 [128, 2048, 1536], P(('head', 'blk')), may hold values from -0.125 to 0.125
- expert_down: bfloat16 [128, 768, 2048], P(('head', 'blk')), may hold values from -0.875 to 0.875
- lengths: int32 [16], replicated, may hold values from 1 to 4096, 16384 in all
- block_deal: int32 [64], replicated, may hold values from 0 to 63, each once
- routes: int32 [16384, 8], P(('head', 'blk')), may hold values from 0 to 127, all different within a row; in each aligned block of 128 rows (0 to 127, 128 to 255, ...) at most 8 rows name the same one
- cotangent: bfloat16 [16384, 2048], P(('head', 'blk')), may hold values from -6 to 6
Outputs:
- output: bfloat16 [16384, 2048], P(('head', 'blk'))
- grad_tokens: float32 [16384, 2048], P(('head', 'blk'))
- grad_norm_gain: float32 [2048], replicated
- grad_w_query: float32 [2048, 4096], P('blk', 'head')
- grad_w_key: float32 [2048, 512], P('blk', 'head')
- grad_w_value: float32 [2048, 512], P('blk', 'head')
- grad_query_gain: float32 [128], replicated
- grad_key_gain: float32 [128], replicated
- grad_w_out: float32 [4096, 2048], P('head', 'blk')
- grad_mix_gain: float32 [2048], replicated
- grad_w_router: float32 [128, 2048], P('head', 'blk')
- grad_expert_gate_up: float32 [128, 2048, 1536], P(('head', 'blk'))
- grad_expert_down: float32 [128, 768, 2048], P(('head', 'blk'))
Inputs may be any that keep to these rules, and one draw needn't show every extreme that they name: `lengths`: they sum to 16384; the largest is exactly 4096. A permutation of the 64 stream blocks of 256 tokens; index b of blk holds block block_deal[b], head index 0 its first 128 tokens. `routes`: each row names 8 different experts; the 128 rows of one device name one expert at most 8 times.
All inputs are finite; a program needn't handle non-finite values.
Results may differ from a plain program's by a relative error of at most 0.03.
Values may be sent and summed in bfloat16 or wider, within the bound.
A program may use at most 704 MiB of HBM per device.

v0:
```python
import math

import jax
import jax.numpy as jnp
from jax import lax
from jax.experimental import pallas as pl
from jax.experimental.pallas import tpu as pltpu
from jax.sharding import PartitionSpec as P

MESH = pl.DeviceIdType.MESH
EPS = 1e-06
ROPE_BASE = 1000000.0
LOG2E = 1.4426950408889634
BF = jnp.bfloat16
F32 = jnp.float32
BLOCK = 256
VMEM_LIMIT = 60 << 20
SIZES = {"zc": 4, "c": 2, "x": 4, "y": 4, "zhc": 4, "z": 8, "yx": 16}


def peers_of(kind):
    h = lax.axis_index("head")
    b = lax.axis_index("blk")
    q, r = lax.div(b, 4), lax.rem(b, 4)
    if kind == "zc":
        return lax.div(r, 2) * 2 + h, lambda g: (lax.rem(g, 2), q * 4 + lax.div(g, 2) * 2 + lax.rem(r, 2))
    if kind == "z":
        return r * 2 + h, lambda g: (lax.rem(g, 2), q * 4 + lax.div(g, 2))
    if kind == "c":
        return lax.rem(b, 2), lambda g: (h, b - lax.rem(b, 2) + g)
    if kind == "x":
        return lax.rem(q, 4), lambda g: (h, (lax.div(q, 4) * 4 + g) * 4 + r)
    if kind == "y":
        return lax.div(q, 4), lambda g: (h, (g * 4 + lax.rem(q, 4)) * 4 + r)
    if kind == "yx":
        return q, lambda g: (h, g * 4 + r)
    return r, lambda g: (h, q * 4 + g)


def cost_of(microseconds):
    return pl.CostEstimate(flops=microseconds * 10**9, bytes_accessed=microseconds * 3 * 10**6, transcendentals=0)


class Flow:
    def __init__(self, inputs, outputs, scratch, partners, steps):
        self.inputs, self.outputs, self.scratch = inputs, outputs, scratch
        self.partners, self.steps = partners, steps


class Filler:
    def __init__(self, cost):
        self.cost = cost


class Clock:
    now = 0.0


def in_turn(flows):
    Clock.now = 0.0
    ready, waiting, fillers = [(0.0, i, steps) for i, steps in enumerate(flows)], [], []
    count = len(flows)
    while ready or fillers or waiting:
        for entry in [e for e in waiting if e[0].ref is not None]:
            waiting.remove(entry)
            ready.append((Clock.now, entry[1], entry[2]))
        ready.sort(key=lambda e: e[:2])
        if fillers and (not ready or ready[0][0] > Clock.now + 0.5):
            cost, order, steps = fillers.pop(0)
            Clock.now += cost
        else:
            when, order, steps = ready.pop(0)
            Clock.now = max(Clock.now, when) + 0.3
        result = next(steps, steps)
        if result is steps:
            continue
        if isinstance(result, Filler):
            fillers.append((result.cost, order, steps))
        elif isinstance(result, Made):
            waiting.append((result, order, steps))
        elif result is None or isinstance(result, float):
            ready.append((Clock.now if result is None else result, order, steps))
        else:
            ready += [(Clock.now, order, steps), (Clock.now, count, result)]
            count += 1


class Made:
    def __init__(self, *shape):
        self.shape, self.ref = shape, None


HOP = 3.0
RATE = 40e3
CORE_RATE = 200e3


def launch(flows, cid, cost):
    partners = sorted({p for flow in flows for p in flow.partners})

    def kernel(*refs):
        n_in, n_out = sum(len(f.inputs) for f in flows), sum(len(f.outputs) for f in flows)
        ins, outs, rest = list(refs[:n_in]), list(refs[n_in : n_in + n_out]), list(refs[n_in + n_out :])
        barrier = pltpu.get_barrier_semaphore()
        for kind, distance in partners:
            me, member = peers_of(kind)
            to = member(lax.rem(me + distance, SIZES[kind]))
            pl.semaphore_signal(barrier, inc=1, device_id=to, device_id_type=MESH)
        running = []
        for flow in flows:
            own = [[group.pop(0) for _ in part] for group, part in ((ins, flow.inputs), (outs, flow.outputs), (rest, flow.scratch))]
            running.append(flow.steps(*own))
            next(running[-1])
        pl.semaphore_wait(barrier, len(partners))
        in_turn(running)

    return pl.pallas_call(
        kernel,
        out_shape=tuple(jax.ShapeDtypeStruct(s, d) for f in flows for s, d, _ in f.outputs),
        in_specs=[pl.BlockSpec(memory_space=space) for f in flows for _, space in f.inputs],
        out_specs=tuple(pl.BlockSpec(memory_space=space) for f in flows for _, _, space in f.outputs),
        scratch_shapes=[x for f in flows for x in f.scratch],
        compiler_params=pltpu.CompilerParams(collective_id=cid, has_side_effects=True, vmem_limit_bytes=VMEM_LIMIT),
        cost_estimate=cost_of(cost),
        name=f"links_{cid}",
    )(*[x for f in flows for x, _ in f.inputs])


def remote(src, dst, send, recv, device):
    return pltpu.make_async_remote_copy(
        src_ref=src, dst_ref=dst, send_sem=send, recv_sem=recv, device_id=device, device_id_type=MESH
    )


def piece(ref, which):
    rows = ref.shape[0] // 2
    return ref.at[pl.ds(which * rows, rows)]


def ring_partners(kind):
    return [(kind, 1), (kind, 3)]


class RingGather:
    def __init__(self, kind, slot, src, send, recv):
        me, member = peers_of(kind)
        up, down = lax.rem(me + 1, 4), lax.rem(me + 3, 4)

        def copy(source, target, i, to):
            return remote(source, target, send.at[i], recv.at[i], member(to))

        mine = slot(me)
        self.copies = [
            copy(piece(src, 0), piece(mine, 0), 0, up),
            copy(piece(src, 1), piece(mine, 1), 1, up),
            copy(piece(src, 1), piece(mine, 1), 2, down),
            copy(piece(src, 0), piece(mine, 0), 3, down),
            copy(piece(slot(down), 0), piece(slot(down), 0), 4, up),
            copy(piece(slot(up), 1), piece(slot(up), 1), 5, down),
        ]

    def start(self):
        for i in (0, 2, 1, 3):
            self.copies[i].start()

    def forward(self):
        self.copies[0].wait_recv()
        self.copies[4].start()
        self.copies[2].wait_recv()
        self.copies[5].start()

    def near(self):
        self.copies[1].wait_recv()
        self.copies[3].wait_recv()

    def far(self):
        self.copies[4].wait_recv()
        self.copies[5].wait_recv()

    def sent(self):
        for copy in self.copies:
            copy.wait_send()


class RingScatter:
    def __init__(self, kind, chunk, bufs, send, recv, raw=None):
        raw = raw or chunk
        self.me, member = peers_of(kind)
        self.up, self.down, self.far = (lax.rem(self.me + k, 4) for k in (1, 3, 2))
        self.chunk, self.bufs = chunk, bufs

        def copy(source, target, i, to):
            return remote(source, bufs.at[target], send.at[i], recv.at[i], member(to))

        self.copies = [
            copy(piece(raw(self.far), 0), 0, 0, self.up),
            copy(piece(raw(self.far), 1), 1, 1, self.down),
            copy(piece(raw(self.up), 1), 2, 2, self.up),
            copy(piece(raw(self.down), 0), 3, 3, self.down),
            copy(bufs.at[6], 4, 4, self.up),
            copy(bufs.at[7], 5, 5, self.down),
        ]

    def start_far(self):
        self.copies[0].start()
        self.copies[1].start()

    def start_up(self):
        self.copies[2].start()

    def start_down(self):
        self.copies[3].start()

    def add(self):
        self.copies[0].wait_recv()
        self.bufs[6] = (piece(self.chunk(self.up), 0)[...].astype(F32) + self.bufs[0].astype(F32)).astype(BF)
        self.copies[4].start()
        self.copies[1].wait_recv()
        self.bufs[7] = (piece(self.chunk(self.down), 1)[...].astype(F32) + self.bufs[1].astype(F32)).astype(BF)
        self.copies[5].start()

    def total(self, which):
        first, second = ((4, 3), (2, 5))[which]
        self.copies[first].wait_recv()
        self.copies[second].wait_recv()
        return self.bufs[first].astype(F32) + self.bufs[second].astype(F32)

    def sent(self):
        for copy in self.copies:
            copy.wait_send()


def dma(*shape):
    return pltpu.SemaphoreType.DMA(shape)


def ring_gather_flow(made):
    shape = (2, 4) + made.shape

    def steps(ins, outs, scratch):
        (out,), src = outs, made.ref
        send, recv, pass_send, pass_recv, local = scratch
        yield
        me, _ = peers_of("zc")
        core, member = peers_of("c")
        ring = RingGather("zc", lambda g: out.at[core, g], src, send, recv)

        def passing(k):
            g = lax.rem(me + k, 4)
            return remote(src if k == 0 else out.at[core, g], out.at[core, g], pass_send.at[k], pass_recv.at[k], member(1 - core))

        passes = [passing(k) for k in range(4)]
        unit = math.prod(made.shape) * 2 / RATE
        begun = Clock.now
        ring.start()
        passes[0].start()
        yield begun + HOP + unit / 2
        ring.forward()
        back = pltpu.make_async_copy(src, out.at[core, me], local.at[0])
        back.start()
        yield begun + HOP + unit
        ring.near()
        passes[1].start()
        passes[3].start()
        yield begun + 2 * HOP + 1.5 * unit
        ring.far()
        passes[2].start()
        yield Clock.now + HOP + 2.0
        back.wait()
        ring.sent()
        for copy in passes:
            copy.wait()

    return Flow(
        [],
        [(shape, BF, pl.ANY)],
        [dma(6), dma(6), dma(4), dma(4), dma(1)],
        ring_partners("zc") + [("c", 1)],
        steps,
    )


def plane_gather_flow(arrays, first, second, ahead=None):
    to_core = ahead is None
    if ahead == "zhc":
        shard = (4, arrays[0][0].shape[0], sum(columns for _, columns, _ in arrays))
    elif ahead == "z":
        shard = (8,) + arrays[0][0].shape
    else:
        shard = arrays.shape
    shape = ((2,) if to_core else ()) + (4, 4) + shard
    n_ahead = SIZES[ahead] if ahead else 1

    def steps(ins, outs, scratch):
        (out,) = outs
        stage, send, recv, pass_send, pass_recv, local, ahead_send, ahead_recv = scratch
        core, member = peers_of("c")
        here, _ = peers_of(first)
        there, _ = peers_of(second)
        view = out.at[core] if to_core else out

        def slot(a, b):
            return view.at[b, a] if first == "x" else view.at[a, b]

        if ahead:
            mine, at = peers_of(ahead)

            def parts(to):
                if ahead == "z":
                    return [(ins[0], stage.at[mine])]
                found, begin = [], 0
                for ref, (_, columns, share) in zip(ins, arrays):
                    source = ref.at[:, pl.ds(pl.multiple_of(lax.div(to, share) * columns, columns), columns)]
                    found.append((source, stage.at[mine, :, pl.ds(begin, columns)]))
                    begin += columns
                return found

            early = [pltpu.make_async_copy(source, target, local.at[i]) for i, (source, target) in enumerate(parts(mine))]
            for k in range(1, n_ahead):
                to = lax.rem(mine + k, n_ahead)
                for i, (source, target) in enumerate(parts(to)):
                    early.append(remote(source, target, ahead_send.at[i, k], ahead_recv.at[i, k], at(to)))
            local_parts = len(parts(mine))
            for copy in early[:local_parts]:
                copy.start()
            yield
            for copy in early[local_parts:]:
                copy.start()
            yield Clock.now + HOP + 7.0
            for copy in early:
                copy.wait()
            src = stage
        else:
            src = arrays.ref
            yield
        ring = RingGather(first, lambda g: slot(g, there), src, send.at[4], recv.at[4])
        columns = [lax.rem(here + k, 4) for k in range(4)]
        rings = [
            RingGather(second, lambda g, a=a: slot(a, g), src if k == 0 else slot(a, there), send.at[k], recv.at[k])
            for k, a in enumerate(columns)
        ]

        def passing(k, m):
            ref = slot(columns[k], lax.rem(there + m, 4))
            return remote(src if k == m == 0 else ref, ref, pass_send.at[k * 4 + m], pass_recv.at[k * 4 + m], member(1 - core))

        passes = {}

        def hand_over(k, m):
            if to_core:
                passes[k, m] = passing(k, m)
                passes[k, m].start()

        unit = math.prod(shard) * 2 / RATE
        begun = Clock.now
        ring.start()
        rings[0].start()
        hand_over(0, 0)
        yield begun + HOP + unit / 2
        ring.forward()
        back = pltpu.make_async_copy(src, slot(here, there), local.at[0])
        back.start()
        yield
        rings[0].forward()
        yield begun + HOP + unit
        ring.near()
        for k in (1, 3):
            rings[k].start()
            hand_over(k, 0)
        yield begun + 2 * HOP + 1.5 * unit
        ring.far()
        rings[2].start()
        hand_over(2, 0)
        yield
        for i, k in enumerate((0, 1, 3, 2)):
            if k > 0:
                yield begun + 2 * HOP + (1.5 * i + 0.5) * unit
                rings[k].forward()
            yield begun + 2 * HOP + (1.5 * i + 1.0) * unit
            rings[k].near()
            hand_over(k, 1)
            hand_over(k, 3)
        for i, k in enumerate((0, 1, 3, 2)):
            yield begun + 3 * HOP + (1.5 * i + 1.5) * unit
            rings[k].far()
            hand_over(k, 2)
        yield Clock.now + HOP
        back.wait()
        ring.sent()
        for one in rings:
            one.sent()
        for copy in passes.values():
            copy.wait()

    return Flow(
        [] if to_core else [(array, pl.ANY) for array, *_ in arrays],
        [(shape, BF, pl.ANY)],
        [pltpu.VMEM((8, 128) if to_core else shard, BF), dma(5, 6), dma(5, 6), dma(16), dma(16), dma(3), dma(3, 8), dma(3, 8)],
        ring_partners("x") + ring_partners("y") + ([("c", 1)] if to_core else []) + [(ahead, k) for k in range(1, n_ahead)],
        steps,
    )


def product_flow(left, right):
    columns, width = left.shape[1], right.shape[1]

    def steps(ins, outs, scratch):
        (out,) = outs
        left_ref, right_ref, local = scratch
        copies = [pltpu.make_async_copy(source, target, local.at[i]) for i, (source, target) in enumerate(zip(ins, (left_ref, right_ref)))]
        for copy in copies:
            copy.start()
        yield
        yield Filler(1.0)
        for copy in copies:
            copy.wait()
        for column in range(0, columns, 256):
            span = slice(column, column + 256)
            out[span, :] = dot_tn(left_ref[:, span], right_ref[...]).astype(BF)
            yield Filler(1.0)

    return Flow(
        [(left, pl.ANY), (right, pl.ANY)],
        [((columns, width), BF, pltpu.VMEM)],
        [pltpu.VMEM(left.shape, BF), pltpu.VMEM(right.shape, BF), dma(2)],
        [],
        steps,
    )


def output_flow(residual, gates, assign, expert_out):
    own, width = residual.shape
    experts = gates.shape[1]
    count = expert_out.shape[0]

    def steps(ins, outs, scratch):
        residual_ref, gates_ref, assign_ref, expert_hbm = ins
        (out,) = outs
        expert_ref, mixing, local = scratch
        copy = pltpu.make_async_copy(expert_hbm, expert_ref, local.at[0])
        copy.start()
        wide = (experts, count)
        cap = count // experts
        spread = (lax.broadcasted_iota(jnp.int32, wide, 1) // cap == lax.broadcasted_iota(jnp.int32, wide, 0)).astype(F32).astype(BF)
        taken = assign_ref[...].astype(F32)
        high = gates_ref[...].astype(BF)
        low = (gates_ref[...] - high.astype(F32)).astype(BF)
        mixing[0] = (dot_nn(high, spread) * taken).astype(BF)
        mixing[1] = (dot_nn(low, spread) * taken).astype(BF)
        yield
        yield Filler(1.0)
        copy.wait()
        for column in range(0, width, 512):
            span = slice(column, column + 512)
            rows = expert_ref[:, span]
            out[:, span] = (residual_ref[:, span] + dot_nn(mixing[0], rows) + dot_nn(mixing[1], rows)).astype(BF)
            yield Filler(1.0)

    return Flow(
        [(residual, pltpu.VMEM), (gates, pltpu.VMEM), (assign, pltpu.VMEM), (expert_out, pl.ANY)],
        [(residual.shape, BF, pltpu.VMEM)],
        [pltpu.VMEM(expert_out.shape, BF), pltpu.VMEM((2, own, count), BF), dma(1)],
        [],
        steps,
    )


sum_partners = [("yx", k) for k in range(1, 16)] + [("z", k) for k in range(1, 8)]


def sum_room(shape):
    return [pltpu.VMEM((16,) + shape, F32), pltpu.VMEM((8,) + shape, F32), pltpu.VMEM(shape, F32), dma(16), dma(16), dma(8), dma(8)]


def sum_steps(src, gains, out, scratch):
    wide, far, middle, sends, recvs, far_sends, far_recvs = scratch
    me, member = peers_of("yx")
    copies = []
    for k in range(1, 16):
        copies.append(remote(src, wide.at[me], sends.at[k], recvs.at[k], member(lax.rem(me + k, 16))))
        copies[-1].start()
    wide[me] = src[...]
    yield Clock.now + HOP + 4.0
    for copy in copies:
        copy.wait()
    middle[...] = jnp.sum(wide[...], axis=0)
    ring, ring_member = peers_of("z")
    late = []
    for k in range(1, 8):
        late.append(remote(middle, far.at[ring], far_sends.at[k], far_recvs.at[k], ring_member(lax.rem(ring + k, 8))))
        late[-1].start()
    far[ring] = middle[...]
    yield Clock.now + HOP + 3.0
    for copy in late:
        copy.wait()
    out[...] = jnp.sum(far[...], axis=0) / gains[1]


def product_scatter_flow(lefts, right, done, units=None, gains=None, key_gain=None):
    arrays = [left for left in lefts if not isinstance(left, Made)]
    own, wide = lefts[0].shape[0] // 8, right.shape[0]
    spans = [0]
    for left in lefts:
        spans.append(spans[-1] + left.shape[1])

    def steps(ins, outs, scratch):
        given = list(ins[: len(arrays)])
        left_refs = [left.ref if isinstance(left, Made) else given.pop(0) for left in lefts]
        right_ref = ins[len(arrays)]
        out, theirs, came, chunks, bufs, send, recv, pass_send, pass_recv, *rest = scratch
        core, member = peers_of("c")
        me, _ = peers_of("zc")
        ring = RingScatter("zc", lambda g: chunks.at[g], bufs, send, recv)

        if units is not None:
            gains_ref = ins[len(arrays) + 1]
            unit_ref = units.ref
            sums, *sum_scratch = rest
            sums[...] = gains_ref[0]
            sums[33:34, :] += key_gain.ref[...]

        def product(c, k, column):
            row = pl.multiple_of((c * 4 + lax.rem(me + k, 4)) * own, own)
            value = sum(
                dot_nt(left_ref[pl.ds(row, own), :], right_ref[column : column + 512, spans[i] : spans[i + 1]])
                for i, left_ref in enumerate(left_refs)
            )
            if units is not None:
                row_sum = jnp.sum(value * unit_ref[pl.ds(row, own), column : column + 512].astype(F32), axis=0, keepdims=True)
                for lane in range(0, 512, 128):
                    at = (column + lane) // 128
                    sums[at : at + 1, :] += row_sum[:, lane : lane + 128]
            return value

        passes = [
            remote(theirs.at[k], came.at[k], pass_send.at[k], pass_recv.at[k], member(1 - core)) for k in range(4)
        ]
        for k in (2, 1, 3, 0):
            if k == 1:
                yield
                Clock.now += 0.7
                passes[2].start()
            for column in range(0, wide, 512):
                theirs[k, :, column : column + 512] = product(1 - core, k, column).astype(BF)
            if k != 2:
                Clock.now += 0.7
                passes[k].start()
                yield
        for k in (2, 1, 3, 0):
            passes[k].wait_recv()
            g = lax.rem(me + k, 4)
            for column in range(0, wide, 512):
                span = slice(column, column + 512)
                value = product(core, k, column) + came[k, :, span].astype(F32)
                if k == 0:
                    out[:, span] = value
                else:
                    chunks[g, :, span] = value.astype(BF)
            Clock.now += 0.7
            if k == 2:
                begun = Clock.now
                ring.start_far()
            elif k == 1:
                ring.start_up()
            elif k == 3:
                ring.start_down()
            yield
        unit = own * wide * 2 / RATE
        if units is not None:
            yield sum_steps(sums, gains_ref, outs[0], sum_scratch)
        yield begun + HOP + unit / 2
        ring.add()
        yield begun + 2 * HOP + 1.5 * unit
        for h in range(2):
            rows = slice(h * own // 2, (h + 1) * own // 2)
            out[rows, :] += ring.total(h)
        done.ref = out
        yield Clock.now + 2.0
        ring.sent()
        for copy in passes:
            copy.wait_send()

    return Flow(
        [(x, pltpu.VMEM) for x in (*arrays, right)] + ([] if units is None else [(gains, pltpu.VMEM)]),
        [] if units is None else [(gains.shape[1:], F32, pltpu.VMEM)],
        [
            pltpu.VMEM((own, wide), F32),
            pltpu.VMEM((4, own, wide), BF),
            pltpu.VMEM((4, own, wide), BF),
            pltpu.VMEM((4, own, wide), BF),
            pltpu.VMEM((8, own // 2, wide), BF),
            dma(6),
            dma(6),
            dma(4),
            dma(4),
        ]
        + ([] if units is None else [pltpu.VMEM(gains.shape[1:], F32)] + sum_room(gains.shape[1:])),
        ring_partners("zc") + [("c", 1)] + ([] if units is None else sum_partners),
        steps,
    )


def plane_scatter_flow(array, first, second, from_core=False, last_in=None):
    rows, columns = array.shape[-2:]
    n_last = SIZES[last_in] if last_in else 1
    result = (n_last, rows // 4, columns) if last_in else (rows, columns)

    def steps(ins, outs, scratch):
        src, (out,) = array.ref if isinstance(array, Made) else ins[0], outs
        came, sums, middle, bufs, late_bufs, send, recv, late_send, late_recv, pass_send, pass_recv, local, cut, cut_send, cut_recv = scratch
        core, member = peers_of("c")
        me, _ = peers_of(first)

        def along(ref, g):
            return ref.at[g] if first == "y" else ref.at[:, g]

        order = [lax.rem(me + k, 4) for k in (2, 1, 3, 0)]
        unit = 4 * rows * columns * 2 / RATE
        loads = [
            pltpu.make_async_copy(along(src.at[core] if from_core else src, g), along(sums, g), local.at[i])
            for i, g in enumerate(order)
            if from_core or i > 0
        ]
        passes = []
        if from_core:
            ring = RingScatter(first, lambda g: along(sums, g), bufs, send, recv)
            for i, g in enumerate(order):
                loads[i].start()
                passes.append(
                    remote(along(src.at[1 - core], g), along(came, g), pass_send.at[i], pass_recv.at[i], member(1 - core))
                )
            yield
            for copy in passes:
                copy.start()
            yield Clock.now + HOP + unit * RATE / CORE_RATE
            starts = [ring.start_far, ring.start_up, ring.start_down, lambda: None]
            for i, g in enumerate(order):
                loads[i].wait()
                passes[i].wait_recv()
                for k in range(4):
                    total = along(sums, g)[k].astype(F32) + along(came, g)[k].astype(F32)
                    along(sums, g)[k] = total.astype(BF)
                starts[i]()
                if i == 0:
                    begun = Clock.now
                yield Clock.now + unit * RATE / CORE_RATE if i < 3 else None
        else:
            ring = RingScatter(first, lambda g: along(sums, g), bufs, send, recv, raw=lambda g: along(src, g))
            for load in loads:
                load.start()
            yield
            begun = Clock.now
            ring.start_far()
            ring.start_up()
            ring.start_down()
            yield begun + HOP + unit / 2
            for load in loads:
                load.wait()
        if from_core:
            yield begun + HOP + unit / 2
        ring.add()
        yield begun + 2 * HOP + 1.5 * unit
        own = along(sums, me)
        for h in range(2):
            came_half = ring.total(h)
            for k in range(2):
                middle[h * 2 + k] = (own[h * 2 + k].astype(F32) + came_half[k]).astype(BF)
        Clock.now += 1.0
        begun = Clock.now
        last = RingScatter(second, lambda g: middle.at[g], late_bufs, late_send, late_recv)
        last.start_far()
        last.start_up()
        last.start_down()
        yield begun + HOP + unit / 8
        last.add()
        yield begun + 2 * HOP + 0.4 * unit
        for h in range(2):
            total = (piece(middle.at[last.me], h)[...].astype(F32) + last.total(h)).astype(BF)
            if last_in:
                cut[2 * h] = total[: rows // 4]
                cut[2 * h + 1] = total[rows // 4 :]
            else:
                out[h * rows // 2 : (h + 1) * rows // 2, :] = total
        cuts = []
        if last_in:
            mine, at = peers_of(last_in)
            share = n_last // 4
            for k in range(1, n_last):
                to = lax.rem(mine + k, n_last)
                cuts.append(remote(cut.at[lax.div(to, share)], out.at[mine], cut_send.at[k], cut_recv.at[k], at(to)))
                cuts[-1].start()
            out[mine] = cut[lax.div(mine, share)]
        yield Clock.now + HOP + 3.0
        ring.sent()
        last.sent()
        for copy in passes:
            copy.wait_send()
        for copy in cuts:
            copy.wait()

    block = (4, 4, rows, columns)
    return Flow(
        [] if isinstance(array, Made) else [(array, pl.ANY)],
        [(result, BF, pltpu.VMEM)],
        [
            pltpu.VMEM(block if from_core else (8, 128), BF),
            pltpu.VMEM(block, BF),
            pltpu.VMEM((4, rows, columns), BF),
            pltpu.VMEM((8, 2, rows, columns), BF),
            pltpu.VMEM((8, rows // 2, columns), BF),
            dma(6),
            dma(6),
            dma(6),
            dma(6),
            dma(4),
            dma(4),
            dma(4),
            pltpu.VMEM((4, rows // 4, columns), BF),
            dma(8),
            dma(8),
        ],
        ring_partners("x")
        + ring_partners("y")
        + ([("c", 1)] if from_core else [])
        + [(last_in, k) for k in range(1, n_last)],
        steps,
    )


def tables_flow(routes, offsets, spacing, experts, cap):
    own, top = routes.shape
    rows, size = offsets.size, spacing.shape[1]

    def steps(ins, outs, scratch):
        routes_ref, offsets_ref, spacing_ref = ins
        assign, chosen_ref, cosine, sine = outs
        yield
        yield Filler(1.0)
        lane = lax.broadcasted_iota(jnp.int32, (own, experts), 1)
        chosen = jnp.zeros((own, experts), F32)
        for k in range(top):
            chosen += (routes_ref[:, k : k + 1] == lane).astype(F32)
        chosen_ref[...] = chosen
        before = lax.broadcasted_iota(jnp.int32, (own, own), 0) > lax.broadcasted_iota(jnp.int32, (own, own), 1)
        earlier = dot_nn(before.astype(F32).astype(BF), chosen.astype(BF))
        wide = (experts, experts * cap)
        spread = (lax.broadcasted_iota(jnp.int32, wide, 1) // cap == lax.broadcasted_iota(jnp.int32, wide, 0)).astype(F32).astype(BF)
        slot = lax.rem(lax.broadcasted_iota(jnp.int32, (own, experts * cap), 1), cap).astype(F32)
        taken = (dot_nn(chosen.astype(BF), spread) > 0.5) & (dot_nn(earlier.astype(BF), spread) == slot)
        assign[...] = taken.astype(F32).astype(BF)
        yield Filler(1.0)
        sign = jnp.where(lax.broadcasted_iota(jnp.int32, (1, size), 1) < size // 2, -1.0, 1.0)
        for row in range(0, rows, BLOCK):
            span = slice(row, row + BLOCK)
            angles = jnp.broadcast_to(offsets_ref[row // BLOCK], (size, BLOCK)).T * spacing_ref[...]
            cosine[span, :] = jnp.cos(angles)
            sine[span, :] = jnp.sin(angles) * sign
            yield Filler(1.0)

    return Flow(
        [(routes, pltpu.VMEM), (offsets, pltpu.VMEM), (spacing, pltpu.VMEM)],
        [
            ((own, experts * cap), BF, pltpu.VMEM),
            ((own, experts), F32, pltpu.VMEM),
            ((rows, size), F32, pltpu.VMEM),
            ((rows, size), F32, pltpu.VMEM),
        ],
        [],
        [],
        steps,
    )


def norm_flow(tokens, gain, made):
    def steps(ins, outs, scratch):
        tokens_ref, gain_ref = ins
        (made.ref,) = scratch
        wide = tokens_ref[...].astype(F32)
        made.ref[...] = (wide * lax.rsqrt(jnp.mean(wide * wide, axis=-1, keepdims=True) + EPS) * gain_ref[...]).astype(BF)
        yield

    return Flow([(tokens, pltpu.VMEM), (gain, pltpu.VMEM)], [], [pltpu.VMEM(tokens.shape, BF)], [], steps)


def project_flow(rows, weights, gain, cosine, sine, q_cols, keys, values):
    count, size = rows.shape[0], gain.shape[1]
    half = count // 2

    def steps(ins, outs, scratch):
        rows_hbm, w_hbm, gain_ref, cos_ref, sin_ref = ins
        q_ref, raw_ref = outs
        rows_ref, w_ref, keys.ref, values.ref, local = scratch
        core, _ = peers_of("c")
        own = pl.ds(pl.multiple_of(core * half, half), half)
        other = pl.ds(pl.multiple_of((1 - core) * half, half), half)
        kv = pl.ds(q_cols, 2 * size)
        copies = [
            pltpu.make_async_copy(w_hbm.at[:, kv], w_ref.at[:, kv], local.at[0]),
            pltpu.make_async_copy(rows_hbm.at[own], rows_ref.at[own], local.at[1]),
            pltpu.make_async_copy(w_hbm.at[:, pl.ds(0, q_cols)], w_ref.at[:, pl.ds(0, q_cols)], local.at[2]),
            pltpu.make_async_copy(rows_hbm.at[other], rows_ref.at[other], local.at[3]),
        ]
        for copy in copies:
            copy.start()
        copies[0].wait()
        copies[1].wait()
        product = dot_nn(rows_ref[own, :], w_ref[:, q_cols:])
        raw = product[:, :size]
        raw_ref[...] = raw
        keys.ref[...] = norm_rope(raw, gain_ref[...], cos_ref[own, :], sin_ref[own, :]).astype(BF)
        values.ref[...] = product[:, size:].astype(BF)
        yield
        yield Filler(1.0)
        copies[2].wait()
        copies[3].wait()
        for row in range(0, count, BLOCK):
            q_ref[row : row + BLOCK, :] = dot_nn(rows_ref[row : row + BLOCK, :], w_ref[:, :q_cols])
            yield Filler(1.2)

    return Flow(
        [(rows, pl.ANY), (weights, pl.ANY), (gain, pltpu.VMEM), (cosine, pltpu.VMEM), (sine, pltpu.VMEM)],
        [((count, q_cols), F32, pltpu.VMEM), ((half, size), F32, pltpu.VMEM)],
        [pltpu.VMEM(rows.shape, BF), pltpu.VMEM(weights.shape, BF), pltpu.VMEM((half, size), BF), pltpu.VMEM((half, size), BF), dma(4)],
        [],
        steps,
    )


def route_flow(tokens, gain, router, chosen, assign, done):
    own, width = tokens.shape
    experts, count = chosen.shape[1], assign.shape[1]

    def steps(ins, outs, scratch):
        tokens_ref, gain_ref, router_ref, chosen_ref, assign_ref = ins
        residual_ref, mixed_ref, gates_ref, rows_ref = outs
        (pick,) = scratch
        yield
        pick[...] = assign_ref[...].T
        yield done
        residual = tokens_ref[...].astype(F32) + done.ref[...]
        residual_ref[...] = residual
        mixed_ref[...] = (residual * lax.rsqrt(jnp.mean(residual * residual, axis=-1, keepdims=True) + EPS) * gain_ref[...]).astype(BF)
        logits = jnp.where(chosen_ref[...] > 0, dot_nn(mixed_ref[...], router_ref[...]), -1e30)
        powers = jnp.exp(logits - jnp.max(logits, axis=-1, keepdims=True))
        gates = powers / jnp.sum(powers, axis=-1, keepdims=True)
        gates_ref[...] = gates
        for column in range(0, width, 512):
            span = slice(column, column + 512)
            rows_ref[:, span] = dot_nn(pick[...], mixed_ref[:, span]).astype(BF)
        rows_ref[:, width:] = dot_nn(pick[...], gates.astype(BF)).astype(BF)
        yield

    return Flow(
        [(x, pltpu.VMEM) for x in (tokens, gain, router, chosen, assign)],
        [
            ((own, width), F32, pltpu.VMEM),
            ((own, width), BF, pltpu.VMEM),
            ((own, experts), F32, pltpu.VMEM),
            ((count, width + experts), BF, pltpu.VMEM),
        ],
        [pltpu.VMEM((count, own), BF)],
        [],
        steps,
    )


def mix_back_flow(back, assign, gates, mixed, router, residual, gain, cotangent, made):
    own, width = mixed.shape
    experts, count = gates.shape[1], back.shape[0]

    def steps(ins, outs, scratch):
        back_hbm, assign_ref, gates_ref, mixed_ref, router_ref, residual_ref, gain_ref, cotangent_ref = ins
        residual_grad, gain_grad, router_grad = outs
        back_ref, mixed_grad, made.ref, local = scratch
        copy = pltpu.make_async_copy(back_hbm, back_ref, local.at[0])
        copy.start()
        copy.wait()
        sums = jnp.sum(back_ref[:, width : width + 128].astype(F32), axis=1, keepdims=True)
        shape = (count, experts)
        expert_of = lax.div(lax.broadcasted_iota(jnp.int32, shape, 0), count // experts)
        spread = jnp.where(expert_of == lax.broadcasted_iota(jnp.int32, shape, 1), sums, 0.0)
        high = spread.astype(BF)
        low = (spread - high.astype(F32)).astype(BF)
        gate_grads = dot_nn(assign_ref[...], high) + dot_nn(assign_ref[...], low)
        gates = gates_ref[...]
        logits_grad = (gates * (gate_grads - jnp.sum(gates * gate_grads, axis=1, keepdims=True))).astype(BF)
        for column in range(0, width, 512):
            span = slice(column, column + 512)
            mixed_grad[:, span] = dot_nn(assign_ref[...], back_ref[:, span]) + dot_nt(logits_grad, router_ref[span, :])
        value = residual_ref[...]
        inverse = lax.rsqrt(jnp.mean(value * value, axis=-1, keepdims=True) + EPS)
        unit = value * inverse
        grad = mixed_grad[...]
        gain_grad[...] = jnp.sum(grad * unit, axis=0, keepdims=True)
        scaled = grad * gain_ref[...]
        total = cotangent_ref[...].astype(F32) + inverse * (scaled - unit * jnp.mean(scaled * unit, axis=-1, keepdims=True))
        residual_grad[...] = total
        made.ref[...] = total.astype(BF)
        yield
        yield Filler(1.0)
        router_grad[...] = dot_tn(mixed_ref[...], logits_grad).astype(BF)
        yield

    return Flow(
        [(back, pl.ANY)] + [(x, pltpu.VMEM) for x in (assign, gates, mixed, router, residual, gain, cotangent)],
        [((own, width), F32, pltpu.VMEM), ((1, width), F32, pltpu.VMEM), ((width, experts), BF, pltpu.VMEM)],
        [pltpu.VMEM(back.shape, BF), pltpu.VMEM((own, width), F32), pltpu.VMEM((own, width), BF), dma(1)],
        [],
        steps,
    )


def key_back_flow(grad_key, grad_value, raw, gain, cosine, sine, units, kv, w_kv, rows, key_gain):
    half, size = raw.shape
    width = units.shape[1]

    def steps(ins, outs, scratch):
        dk_ref, dv_ref, raw_ref, gain_ref, cos_ref, sin_ref, units_hbm = ins
        rows.ref, kv.ref, w_kv.ref, key_gain.ref, local = scratch
        copy = pltpu.make_async_copy(units_hbm, rows.ref, local.at[0])
        copy.start()
        core, _ = peers_of("c")
        own = pl.ds(pl.multiple_of(core * half, half), half)
        grad = dk_ref[...].astype(F32)
        grad_raw, grad_gain = norm_rope_back(grad, raw_ref[...], gain_ref[...], cos_ref[own, :], sin_ref[own, :])
        kv.ref[...] = jnp.zeros(kv.shape, BF)
        kv.ref[own, :size] = grad_raw.astype(BF)
        kv.ref[own, size:] = dv_ref[...]
        key_gain.ref[...] = jnp.sum(grad_gain, axis=0, keepdims=True)
        copy.wait()
        for i in range(16):
            w_kv.ref[i // 4, i % 4] = dot_tn(rows.ref[own, i * width // 16 : (i + 1) * width // 16], kv.ref[own, :]).astype(BF)
        yield

    return Flow(
        [(x, pltpu.VMEM) for x in (grad_key, grad_value, raw, gain, cosine, sine)] + [(units, pl.ANY)],
        [],
        [pltpu.VMEM(rows.shape, BF), pltpu.VMEM(kv.shape, BF), pltpu.VMEM(w_kv.shape, BF), pltpu.VMEM((1, size), F32), dma(1)],
        [],
        steps,
    )


def tokens_grad_flow(tokens, gain, residual_grad, done):
    def steps(ins, outs, scratch):
        tokens_ref, gain_ref, residual_ref = ins
        (out,) = outs
        yield
        yield done
        value = tokens_ref[...].astype(F32)
        inverse = lax.rsqrt(jnp.mean(value * value, axis=-1, keepdims=True) + EPS)
        unit = value * inverse
        scaled = done.ref[...] * gain_ref[...]
        out[...] = residual_ref[...] + inverse * (scaled - unit * jnp.mean(scaled * unit, axis=-1, keepdims=True))
        yield

    return Flow(
        [(x, pltpu.VMEM) for x in (tokens, gain, residual_grad)], [(tokens.shape, F32, pltpu.VMEM)], [], [], steps
    )


def add_up(stacked):
    return jnp.sum(stacked.astype(F32), axis=0)


def dot_nn(a, b):
    return lax.dot_general(a, b, (((1,), (0,)), ((), ())), preferred_element_type=F32)


def dot_nt(a, b):
    return lax.dot_general(a, b, (((1,), (1,)), ((), ())), preferred_element_type=F32)


def dot_tn(a, b):
    return lax.dot_general(a, b, (((0,), (0,)), ((), ())), preferred_element_type=F32)


def norm_rope(raw, gain, cosine, sine):
    unit = raw * lax.rsqrt(jnp.mean(raw * raw, axis=-1, keepdims=True) + EPS)
    scaled = unit * gain
    return scaled * cosine + pltpu.roll(scaled, 64, 1) * sine


def norm_rope_back(grad, raw, gain, cosine, sine):
    inverse = lax.rsqrt(jnp.mean(raw * raw, axis=-1, keepdims=True) + EPS)
    unit = raw * inverse
    turned = grad * cosine + pltpu.roll(grad * sine, 64, 1)
    scaled = turned * gain
    return inverse * (scaled - unit * jnp.mean(scaled * unit, axis=-1, keepdims=True)), turned * unit


def expert_kernel(rows_ref, plain_ref, w_ref, back_ref, hidden_ref, gated_ref, both_ref):
    width, ff = w_ref.shape[0], plain_ref.shape[1]
    own = lax.axis_index("head") * lax.axis_size("blk") + lax.axis_index("blk")
    gates = rows_ref[:, width:].astype(F32)
    lane = lax.broadcasted_iota(jnp.int32, gates.shape, 1)
    gate = jnp.sum(jnp.where(lane == own, gates, 0.0), axis=1, keepdims=True)
    gate_up = dot_nn(rows_ref[:, :width], w_ref[...])
    first, up = gate_up[:, :ff], gate_up[:, ff:]
    sigma = 1.0 / (1.0 + jnp.exp(-first))
    silu = first * sigma
    hidden = silu * up
    hidden_ref[...] = hidden.astype(BF)
    gated_ref[...] = (hidden * gate).astype(BF)
    plain = plain_ref[...]
    gate_grad = jnp.sum(hidden * plain, axis=1, keepdims=True)
    grad = plain * gate
    both_ref[:, :ff] = (grad * up * (sigma * (1.0 + first * (1.0 - sigma)))).astype(BF)
    both_ref[:, ff:] = (grad * silu).astype(BF)
    back_ref[:, :width] = dot_nt(both_ref[...], w_ref[...]).astype(BF)
    high = gate_grad.astype(BF).astype(F32)
    back_ref[:, width:] = jnp.where(lane == 0, high, jnp.where(lane == 1, gate_grad - high, 0.0)).astype(BF)


def key_tiles(lo, full, last, tiles):
    middle = jnp.minimum(full, last)
    fours = lax.div(last - middle, 4)
    rest = middle + 4 * fours
    pl.loop(lo, middle)(lambda t: tiles([t], True))
    pl.loop(0, fours)(lambda i: tiles([middle + 4 * i + n for n in range(4)], False))
    pl.loop(rest, last)(lambda t: tiles([t], False))
    tiles([last], True)


def stacked(ref, slots):
    return ref[slots[0]] if len(slots) == 1 else jnp.concatenate([ref[slot] for slot in slots], axis=0)


def allowed_pairs(t, last, start, shape):
    key_place = t * BLOCK + lax.broadcasted_iota(jnp.int32, shape, 0)
    query_place = last * BLOCK + lax.rem(lax.broadcasted_iota(jnp.int32, shape, 1), BLOCK)
    return (key_place >= start) & (key_place <= query_place)


def attend_forward_kernel(
    lo_ref, full_ref, last_ref, slot_ref, raw_ref, gain_ref, cos_ref, sin_ref, k_ref, v_ref, start_ref, q_ref, o_ref, log_ref, q_t, acc, total
):
    j = pl.program_id(0)
    size = k_ref.shape[2]
    heads = raw_ref.shape[1] // size
    scale = size**-0.5 * LOG2E
    last = last_ref[j]
    for n in range(heads):
        span = slice(n * size, (n + 1) * size)
        query = norm_rope(raw_ref[:, span], gain_ref[...], cos_ref[...], sin_ref[...])
        q_ref[:, span] = query.astype(BF)
        q_t[:, n * BLOCK : (n + 1) * BLOCK] = query.T.astype(BF)
    acc[...] = jnp.zeros_like(acc)
    total[...] = jnp.zeros_like(total)
    start = start_ref[0]

    def tiles(at, masked):
        slots = [slot_ref[t] for t in at]
        weights = jnp.exp2(dot_nn(stacked(k_ref, slots), q_t[...]) * scale)
        if masked:
            weights = jnp.where(allowed_pairs(at[0], last, start, weights.shape), weights, 0.0)
        total[...] += jnp.sum(weights.reshape(-1, 8, heads * BLOCK), axis=0)
        acc[...] += dot_nn(stacked(v_ref, slots).T, weights.astype(BF))

    key_tiles(lo_ref[j], full_ref[j], last, tiles)
    row = jnp.sum(total[...], axis=0, keepdims=True)
    log_ref[0] = jnp.log2(row)
    out = acc[...] / row
    for n in range(heads):
        o_ref[:, n * size : (n + 1) * size] = out[:, n * BLOCK : (n + 1) * BLOCK].T.astype(BF)


def attend_backward_kernel(
    lo_ref,
    full_ref,
    last_ref,
    slot_ref,
    raw_ref,
    gain_ref,
    cos_ref,
    sin_ref,
    k_ref,
    v_ref,
    start_ref,
    q_ref,
    o_ref,
    g_ref,
    w_ref,
    log_ref,
    dq_ref,
    sum_ref,
    dk_ref,
    dv_ref,
    queries,
    q_t,
    grads,
    g_t,
    delta,
    acc,
    dk,
    dv,
    keys_ref,
    values_ref,
    local,
):
    j = pl.program_id(0)
    slots, _, size = keys_ref.shape
    takes = [pltpu.make_async_copy(k_ref, keys_ref, local.at[0]), pltpu.make_async_copy(v_ref, values_ref, local.at[1])]
    heads = raw_ref.shape[1] // size
    scale = size**-0.5
    last = last_ref[j]

    @pl.when(j == 0)
    def _():
        for copy in takes:
            copy.start()
        sum_ref[...] = jnp.zeros_like(sum_ref)

        @pl.loop(0, slots)
        def _(s):
            dk[s] = jnp.zeros(dk.shape[1:], F32)
            dv[s] = jnp.zeros(dv.shape[1:], F32)

    attended_grad = dot_nn(g_ref[...], w_ref[...]).astype(BF)
    for n in range(heads):
        span, rows = slice(n * size, (n + 1) * size), slice(n * BLOCK, (n + 1) * BLOCK)
        queries[rows, :] = q_ref[:, span]
        q_t[:, rows] = q_ref[:, span].T
        grads[rows, :] = attended_grad[:, span]
        grad_t = attended_grad[:, span].T
        g_t[:, rows] = grad_t
        delta[:, rows] = jnp.sum(grad_t.astype(F32) * o_ref[:, span].T.astype(F32), axis=0, keepdims=True)
    acc[...] = jnp.zeros_like(acc)
    start = start_ref[0]
    logs = log_ref[0]

    @pl.when(j == 0)
    def _():
        for copy in takes:
            copy.wait()

    def tiles(at, masked):
        slots = [slot_ref[t] for t in at]
        keys = stacked(keys_ref, slots)
        probs = jnp.exp2(dot_nn(keys, q_t[...]) * (scale * LOG2E) - logs)
        if masked:
            probs = jnp.where(allowed_pairs(at[0], last, start, probs.shape), probs, 0.0)
        grad_scores = (probs * (dot_nn(stacked(values_ref, slots), g_t[...]) - delta[...])).astype(BF)
        values_part, keys_part = dot_nn(probs.astype(BF), grads[...]), dot_nn(grad_scores, queries[...])
        for n, slot in enumerate(slots):
            dv[slot] += values_part[n * BLOCK : (n + 1) * BLOCK]
            dk[slot] += keys_part[n * BLOCK : (n + 1) * BLOCK]
        acc[...] += dot_nn(keys.T, grad_scores)

    key_tiles(lo_ref[j], full_ref[j], last, tiles)
    for n in range(heads):
        span = slice(n * size, (n + 1) * size)
        grad = (acc[:, n * BLOCK : (n + 1) * BLOCK] * scale).T.astype(BF).astype(F32)
        grad_raw, grad_gain = norm_rope_back(grad, raw_ref[:, span], gain_ref[...], cos_ref[...], sin_ref[...])
        dq_ref[:, span] = grad_raw.astype(BF)
        sum_ref[...] += jnp.sum(grad_gain, axis=0, keepdims=True)

    @pl.when(j == pl.num_programs(0) - 1)
    def _():
        def out(s, n):
            span = pl.ds(s, n)
            return (
                pltpu.make_async_copy(keys_ref.at[span], dk_ref.at[span], local.at[0]),
                pltpu.make_async_copy(values_ref.at[span], dv_ref.at[span], local.at[1]),
            )

        @pl.loop(0, slots, step=8)
        def _(s):
            for i in range(8):
                keys_ref[s + i] = (dk[s + i] * scale).astype(BF)
                values_ref[s + i] = dv[s + i].astype(BF)
            for copy in out(s, 8):
                copy.start()

        for copy in out(0, slots):
            copy.wait()


def by_rows(array, rows=BLOCK):
    return pl.BlockSpec((rows,) + array.shape[1:], lambda j, *_: (j,) + (0,) * (array.ndim - 1))


def resident(array):
    return pl.BlockSpec(array.shape, lambda j, *_: (0,) * array.ndim, pipeline_mode=pl.Buffered(1))


def shaped(shape, dtype):
    return jax.ShapeDtypeStruct(shape, dtype)


def expert(rows, plain, weights, block=512):
    count, ff = plain.shape
    outs = (shaped(rows.shape, BF), shaped((count, ff), BF), shaped((count, ff), BF), shaped((count, 2 * ff), BF))
    return pl.pallas_call(
        expert_kernel,
        out_shape=outs,
        grid=(count // block,),
        in_specs=[by_rows(rows, block), by_rows(plain, block), resident(weights)],
        out_specs=tuple(by_rows(x, block) for x in outs),
        compiler_params=pltpu.CompilerParams(vmem_limit_bytes=VMEM_LIMIT),
        cost_estimate=cost_of(20),
        name="expert",
    )(rows, plain, weights)


def attend_forward(meta, raw, gain, cosine, sine, keys, values, start):
    rows, wide = raw.shape
    blocks, size = rows // BLOCK, keys.shape[2]
    lanes = wide // size * BLOCK
    outs = (shaped((rows, wide), BF), shaped((rows, wide), BF), shaped((blocks, 1, lanes), F32))
    return pl.pallas_call(
        attend_forward_kernel,
        out_shape=outs,
        grid_spec=pltpu.PrefetchScalarGridSpec(
            num_scalar_prefetch=4,
            grid=(blocks,),
            in_specs=[
                by_rows(raw),
                resident(gain),
                by_rows(cosine),
                by_rows(sine),
                resident(keys),
                resident(values),
                by_rows(start, 1),
            ],
            out_specs=(by_rows(outs[0]), by_rows(outs[1]), by_rows(outs[2], 1)),
            scratch_shapes=[pltpu.VMEM((size, lanes), BF), pltpu.VMEM((size, lanes), F32), pltpu.VMEM((8, lanes), F32)],
        ),
        compiler_params=pltpu.CompilerParams(vmem_limit_bytes=VMEM_LIMIT),
        cost_estimate=cost_of(30),
        name="attend",
    )(*meta, raw, gain, cosine, sine, keys, values, start)


def attend_backward(meta, raw, gain, cosine, sine, keys, values, start, queries, attended, grads, w_out_t, logs):
    rows, wide = raw.shape
    blocks, size = rows // BLOCK, keys.shape[2]
    lanes = wide // size * BLOCK
    outs = (shaped((rows, wide), BF), shaped((1, size), F32), shaped(keys.shape, BF), shaped(values.shape, BF))
    return pl.pallas_call(
        attend_backward_kernel,
        out_shape=outs,
        grid_spec=pltpu.PrefetchScalarGridSpec(
            num_scalar_prefetch=4,
            grid=(blocks,),
            in_specs=[
                by_rows(raw),
                resident(gain),
                by_rows(cosine),
                by_rows(sine),
                pl.BlockSpec(memory_space=pl.ANY),
                pl.BlockSpec(memory_space=pl.ANY),
                by_rows(start, 1),
                by_rows(queries),
                by_rows(attended),
                by_rows(grads),
                resident(w_out_t),
                by_rows(logs, 1),
            ],
            out_specs=(by_rows(outs[0]), resident(outs[1])) + (pl.BlockSpec(memory_space=pl.ANY),) * 2,
            scratch_shapes=[
                pltpu.VMEM((lanes, size), BF),
                pltpu.VMEM((size, lanes), BF),
                pltpu.VMEM((lanes, size), BF),
                pltpu.VMEM((size, lanes), BF),
                pltpu.VMEM((1, lanes), F32),
                pltpu.VMEM((size, lanes), F32),
                pltpu.VMEM(keys.shape, F32),
                pltpu.VMEM(values.shape, F32),
                pltpu.VMEM(keys.shape, BF),
                pltpu.VMEM(values.shape, BF),
                dma(2),
            ],
        ),
        compiler_params=pltpu.CompilerParams(vmem_limit_bytes=VMEM_LIMIT),
        cost_estimate=cost_of(40),
        name="attend_back",
    )(*meta, raw, gain, cosine, sine, keys, values, start, queries, attended, grads, w_out_t, logs)


def all_to_all(stacked):
    return lax.all_to_all(stacked, ("head", "blk"), split_axis=0, concat_axis=0, tiled=True)


def body(
    tokens,
    norm_gain,
    w_query,
    key_weight,
    value_weight,
    query_gain,
    key_gain,
    w_out,
    mix_gain,
    w_router,
    expert_gate_up,
    expert_down,
    lengths,
    block_deal,
    routes,
    cotangent,
):
    own, width = tokens.shape
    size = query_gain.shape[0]
    scale = size ** (-0.5)
    blk = lax.axis_index("blk")
    plane, core = blk // 4, blk % 2
    devices = lax.axis_size("head") * lax.axis_size("blk")
    experts = w_router.shape[0] * 2
    cap = own * routes.shape[1] // experts
    gate_up, down = expert_gate_up[0], expert_down[0]
    ff = down.shape[0]
    group_rows = 8 * own
    q_cols = w_query.shape[1] // 4
    heads = q_cols // size

    group_blocks = plane * 4 + jnp.array([0, 2, 1, 3], jnp.int32)
    ids = jnp.arange(block_deal.shape[0], dtype=jnp.int32)
    last = jnp.sum(jnp.where(group_blocks[:, None] == ids[None, :], block_deal[None, :], 0), axis=1)
    slots = (ids % 2) * (ids.shape[0] // 2) + (ids // 4) * 2 + (ids % 4) // 2
    slot_of = jnp.sum(jnp.where(block_deal[None, :] == ids[:, None], slots[None, :], 0), axis=1)
    place = (last[:, None] * BLOCK + jnp.arange(BLOCK, dtype=jnp.int32)[None, :]).reshape(-1)
    passed = place[:, None] >= jnp.cumsum(lengths)[None, :]
    start = jnp.sum(jnp.where(passed, lengths[None, :], 0), axis=1)
    start_rows = start.reshape(-1, 1, BLOCK)
    meta = (start_rows[:, 0, 0] // BLOCK, (start_rows[:, 0, BLOCK - 1] + BLOCK - 1) // BLOCK, last, slot_of)
    start_rows = jnp.tile(start_rows, (1, 1, heads))
    offsets = (place - start).astype(F32).reshape(-1, 1, BLOCK)
    spacing = ROPE_BASE ** (-2.0 * jnp.arange(size // 2, dtype=F32) / size)
    spacing = jnp.concatenate([spacing, spacing])[None]

    normed = Made(own, width)
    depth = w_query.shape[0]
    out_pack = w_out.reshape(4, q_cols, depth).transpose(2, 0, 1).reshape(depth, -1)
    side = lax.axis_index("head") == jnp.arange(2, dtype=jnp.int32)
    router_pack = jnp.where(side[None, :, None], w_router.T[:, None, :], 0).astype(BF).reshape(depth, experts)
    w_qkv, w_out_t, w_router_t, group_tokens, assign_low, chosen, cosine, sine = launch(
        [
            norm_flow(tokens, norm_gain[None], normed),
            plane_gather_flow([(w_query, q_cols, 1), (key_weight, size, 2), (value_weight, size, 2)], "x", "y", ahead="zhc"),
            plane_gather_flow([(out_pack, q_cols, 1)], "y", "x", ahead="zhc"),
            plane_gather_flow([(router_pack, experts, 1)], "y", "x", ahead="z"),
            ring_gather_flow(normed),
            tables_flow(routes, offsets, spacing, experts, cap),
        ],
        0,
        45,
    )
    normed_group = group_tokens.reshape(group_rows, width)
    w_qkv, w_out_t = w_qkv.reshape(width, -1), w_out_t.reshape(width, -1)
    w_router_t = jnp.sum(w_router_t.reshape(-1, 2, depth, experts), axis=1).reshape(width, experts)

    q_gain, k_gain = query_gain[None], key_gain[None]
    key, value = Made(group_rows // 2, size), Made(group_rows // 2, size)
    q_raw, k_raw, keys, values, grad_rows = launch(
        [
            project_flow(normed_group, w_qkv, k_gain, cosine, sine, q_cols, key, value),
            plane_gather_flow(key, "x", "y"),
            plane_gather_flow(value, "y", "x"),
            product_flow(assign_low, cotangent),
        ],
        1,
        35,
    )
    grad_rows = all_to_all(grad_rows.reshape(devices, cap, width)).reshape(-1, width)
    keys, values = keys.reshape(-1, BLOCK, size), values.reshape(-1, BLOCK, size)
    queries, attended, logs = attend_forward(meta, q_raw, q_gain, cosine, sine, keys, values, start_rows)

    attention = Made(own, width)
    residual, mixed, gates, outgoing = launch(
        [
            product_scatter_flow([attended], w_out_t, attention),
            route_flow(tokens, mix_gain[None], w_router_t, chosen, assign_low, attention),
        ],
        2,
        30,
    )
    outgoing, grad_rows = lax.optimization_barrier((outgoing, grad_rows))
    arrived = all_to_all(outgoing.reshape(devices, cap, -1)).reshape(experts * cap, -1)

    plain_grad = lax.optimization_barrier(dot_nt(grad_rows, down))
    rows, plain_grad = lax.optimization_barrier((arrived, plain_grad))
    back, hidden, gated, grad_both = expert(rows, plain_grad, gate_up)
    back = all_to_all(back.reshape(devices, cap, -1)).reshape(experts * cap, -1)
    back, expert_out = lax.optimization_barrier((back, dot_nn(hidden, down).astype(BF)))
    grad_down = dot_tn(gated, grad_rows)
    grad_gate_up = dot_tn(rows[:, :width], grad_both)

    grad_attention = Made(own, width)
    grad_residual, grad_mix_gain, grad_router_t, grad_group = launch(
        [
            mix_back_flow(back, assign_low, gates, mixed, w_router_t, residual, mix_gain[None], cotangent, grad_attention),
            ring_gather_flow(grad_attention),
        ],
        3,
        25,
    )
    grad_group = grad_group.reshape(group_rows, width)
    grad_group, expert_out = lax.optimization_barrier((grad_group, expert_out))
    expert_out = all_to_all(expert_out.reshape(devices, cap, width)).reshape(-1, width)
    grad_q, grad_query_gain, grad_keys, grad_values = attend_backward(
        meta, q_raw, q_gain, cosine, sine, keys, values, start_rows, queries, attended, grad_group, w_out_t, logs
    )

    split = (2, 4, 4, group_rows // 2, size)
    grad_key, grad_value, grad_wq, grad_wo = launch(
        [
            plane_scatter_flow(grad_keys.reshape(split), "y", "x", from_core=True),
            plane_scatter_flow(grad_values.reshape(split), "x", "y", from_core=True),
            product_flow(normed_group, grad_q),
            product_flow(grad_group, attended),
        ],
        4,
        35,
    )

    grad_key, expert_out = lax.optimization_barrier((grad_key, expert_out))
    plane_split = (4, 4, 4 * depth, -1)
    zeros, ones = jnp.zeros((width,), F32), jnp.ones((width,), F32)
    gains = jnp.concatenate([zeros, grad_mix_gain[0], grad_query_gain[0], zeros[: 7 * size], norm_gain, ones, ones[: 8 * size]])
    units, grad_kv, grad_wkv, key_gain_sum = Made(group_rows, width), Made(group_rows, 2 * size), Made(4, 4, 4 * depth, 2 * size), Made()
    grad_normed = Made(own, width)
    grad_wq, grad_wo, gains, grad_wkv, grad_wr, output, grad_tokens = launch(
        [
            key_back_flow(grad_key, grad_value, k_raw, k_gain, cosine, sine, normed_group, grad_kv, grad_wkv, units, key_gain_sum),
            plane_scatter_flow(grad_wq.reshape(plane_split), "y", "x", last_in="zhc"),
            plane_scatter_flow(grad_wo.reshape(plane_split), "x", "y", last_in="zhc"),
            product_scatter_flow([grad_q, grad_kv], w_qkv, grad_normed, units, gains.reshape(2, -1, size), key_gain_sum),
            plane_scatter_flow(grad_wkv, "y", "x", last_in="zhc"),
            plane_scatter_flow(grad_router_t.reshape(plane_split), "x", "y", last_in="z"),
            output_flow(residual, gates, assign_low, expert_out),
            tokens_grad_flow(tokens, norm_gain[None], grad_residual, grad_normed),
        ],
        5,
        50,
    )
    gains = gains.reshape(-1)
    grad_w_query = grad_wq.astype(F32).transpose(1, 0, 2).reshape(depth, -1)
    grad_kv_w = jnp.sum(grad_wkv.astype(F32).reshape(2, 2, depth, 2, size), axis=1)
    grad_w_key = grad_kv_w[:, :, 0].transpose(1, 0, 2).reshape(depth, -1)
    grad_w_value = grad_kv_w[:, :, 1].transpose(1, 0, 2).reshape(depth, -1)
    grad_w_out = grad_wo.astype(F32).transpose(0, 2, 1).reshape(-1, depth)
    grad_w_router = lax.dynamic_slice_in_dim(add_up(grad_wr), lax.axis_index("head") * (experts // 2), experts // 2, 1).T
    return (
        output,
        grad_tokens,
        gains[:width],
        grad_w_query,
        grad_w_key,
        grad_w_value,
        gains[2 * width : 2 * width + size],
        gains[2 * width + size : 2 * width + 2 * size],
        grad_w_out,
        gains[width : 2 * width],
        grad_w_router,
        grad_gate_up[None],
        grad_down[None],
    )


def solution(mesh):
    rows, both = P(("head", "blk"), None), P("blk", "head")
    expert, turned = P(("head", "blk"), None, None), P("head", "blk")
    in_specs = (rows, P(), both, both, both, P(), P(), turned, P(), turned, expert, expert, P(), P(), rows, rows)
    out_specs = (rows, rows, P(), both, both, both, P(), P(), turned, P(), turned, expert, expert)
    return jax.shard_map(body, mesh=mesh, in_specs=in_specs, out_specs=out_specs, check_vma=False)
```

profile of v0, /device:TPU:1, one launch (start us, length us, event | category | flops | bytes accessed | tf_op | source)
XLA Modules:
  0.0 530.4 jit_solution(16951392372030758988)
XLA Ops:
  0.7 0.8 broadcast_add_fusion
  1.5 0.9 select_reduce_fusion.2.last_ref
  3.4 1.0 reshape.283
  6.1 1.4 copy.47.refs_7_
  10.1 58.4 %links_0.1 = (bf16[4,4,4,32,768]{4,3,2,1,0:T(8,128)(2,1)}, bf16[4,4,4,32,512]{4,3,2,1,0:T(8,128)(2,1)}, bf16[4,4,8,32,128]{4,3,2,1,0:T(8,128)(2,1)}, bf16[2,4,12...) custom-call(bf16[128,2048]{1,0:T(8,128)(2,1)} %refs_17_.1, ...), custom_call_target="tpu_custom_call" | custom-call | flops 44999999488 | bytes 135000000 | tf_op jit(solution)/shard_map/links_0/pallas_call | solution.py:117
  68.5 37.8 %links_1.1 = (f32[1024,512]{1,0:T(8,128)}, f32[512,128]{1,0:T(8,128)}, bf16[2,4,4,512,128]{4,3,2,1,0:T(8,128)(2,1)}, bf16[2,4,4,512,128]{4,3,2,1,0:T(8,128)(2,1)}, bf16[1024,2048]{1,0:T(8,128)(2,1)}) custom-call(bf16[1024,2048]{1,0:T(8,128)(2,1)} %bitcast.124, bf16[2048,768]{1,0:T(8,128)(2,1)} %bitcast.135, f32[1,128]{1,0:T(1,128)} %bitcast.122, ...), custom_call_target="tpu_custom_call" | custom-call | flops 35000000512 | bytes 105000000 | tf_op jit(solution)/shard_map/links_1/pallas_call | solution.py:117
  106.3 6.8 %all-to-all-start = ((bf16[128,8,2048]{2,1,0:T(8,128)(2,1)}), bf16[128,8,2048]{2,1,0:T(8,128)(2,1)}, u32[]{:S(2)}, u32[]{:S(2)}) async-start(bf16[128,8,2048]{2,1,0:T(8,128)(2,1)} %bitcast.98), calls=%async_computation | async-start | bytes 8388608 | tf_op jit(solution)/shard_map/all_to_all | solution.py:1282
  115.3 19.0 %attend.1 = (bf16[1024,512]{1,0:T(8,128)(2,1)}, bf16[1024,512]{1,0:T(8,128)(2,1)}, f32[4,1,1024]{2,1,0:T(1,128)}) custom-call(s32[4]{0:T(128)} %get-tuple-element.128.lo_ref, s32[4]{0:T(128)} %get-tuple-element.127.full_ref, s32[4]{0:T(128)} %copy-done.7, s32[64]{0:T(128)} %select_reduce_fusion.1.slot_ref, f32[1024,512]{1,0:T(8,128)} %get-tuple-element.71.raw_ref, ...), custom_call_target="tpu_custom_call" | custom-call | flops 30000001024 | bytes 90000000 | tf_op jit(solution)/shard_map/attend/pallas_call | solution.py:1211
  134.3 2.3 reduce_sum.60
  136.6 47.5 %links_2.1 = (f32[128,2048]{1,0:T(8,128)}, bf16[128,2048]{1,0:T(8,128)(2,1)}, f32[128,128]{1,0:T(8,128)}, bf16[1024,2176]{1,0:T(8,128)(2,1)}) custom-call(bf16[1024,512]{1,0:T(8,128)(2,1)} %get-tuple-element.75.refs_0_.o_ref.refs_5_, bf16[2048,512]{1,0:T(8,128)(2,1)} %bitcast.137, bf16[128,2048]{1,0:T(8,128)(2,1)} %refs_17_.1, f32[1,2048]{1,0:T(1,128)} %bitcast.118, ...), custom_call_target="tpu_custom_call" | custom-call | flops 30000001024 | bytes 90000000 | tf_op jit(solution)/shard_map/links_2/pallas_call | solution.py:117
  184.2 9.6 %all-to-all-start.1 = ((bf16[128,8,2176]{2,1,0:T(8,128)(2,1)}), bf16[128,8,2176]{2,1,0:T(8,128)(2,1)}, u32[]{:S(2)}, u32[]{:S(2)}) async-start(bf16[128,8,2176]{2,1,0:T(8,128)(2,1)} %bitcast.96), calls=%async_computation.1 | async-start | bytes 8912896 | tf_op jit(solution)/shard_map/all_to_all | solution.py:1282
  193.8 7.3 %fusion.2.plain_ref = f32[1024,768]{1,0:T(8,128)} fusion(bf16[1024,2048]{1,0:T(8,128)(2,1)} %bitcast.17, bf16[1,768,2048]{2,1,0:T(8,128)(2,1)S(1)} %copy-done), kind=kOutput, calls=%fused_computation.5 | convolution fusion | flops 3221225472 | bytes 10485760 | tf_op jit(solution)/shard_map/dot_general | solution.py:971
  201.1 48.2 %all-to-all-done.1 = bf16[128,8,2176]{2,1,0:T(8,128)(2,1)} async-done(((bf16[128,8,2176]{2,1,0:T(8,128)(2,1)}), bf16[128,8,2176]{2,1,0:T(8,128)(2,1)}, u32[]{:S(2)}, u32[]{:S(2)}) %all-to-all-start.1) | async-done | bytes 4456480 | tf_op jit(solution)/shard_map/all_to_all | solution.py:1282
  249.3 19.2 %expert.1 = (bf16[1024,2176]{1,0:T(8,128)(2,1)}, bf16[1024,768]{1,0:T(8,128)(2,1)}, bf16[1024,768]{1,0:T(8,128)(2,1)}, bf16[1024,1536]{1,0:T(8,128)(2,1)}) custom-call(bf16[1024,2176]{1,0:T(8,128)(2,1)} %bitcast.19.rows_ref, f32[1024,768]{1,0:T(8,128)} %fusion.2.plain_ref, bf16[2048,1536]{1,0:T(8,128)(2,1)} %bitcast.117), custom_call_target="tpu_custom_call" | custom-call | flops 20000000000 | bytes 60000000 | tf_op jit(solution)/shard_map/expert/pallas_call | solution.py:1194
  268.6 11.3 %all-to-all-start.2 = ((bf16[128,8,2176]{2,1,0:T(8,128)(2,1)}), bf16[128,8,2176]{2,1,0:T(8,128)(2,1)}, u32[]{:S(2)}, u32[]{:S(2)}) async-start(bf16[128,8,2176]{2,1,0:T(8,128)(2,1)} %bitcast.95), calls=%async_computation.2 | async-start | bytes 8912896 | tf_op jit(solution)/shard_map/all_to_all | solution.py:1282
  279.9 6.5 %convolution_convert_fusion = bf16[1024,2048]{1,0:T(8,128)(2,1)} fusion(bf16[1024,768]{1,0:T(8,128)(2,1)} %get-tuple-element.86, bf16[1,768,2048]{2,1,0:T(8,128)(2,1)S(1)} %copy-done), kind=kOutput, calls=%fused_computation.3 | convolution fusion | flops 3223322624 | bytes 8912896 | tf_op jit(solution)/shard_map/dot_general | solution.py:967
  286.4 7.7 %convolution_bitcast_fusion.1 = f32[1,768,2048]{2,1,0:T(8,128)} fusion(bf16[1024,768]{1,0:T(8,128)(2,1)S(1)} %copy-done.2, bf16[1024,2048]{1,0:T(8,128)(2,1)} %bitcast.17), kind=kOutput, calls=%fused_computation.2 | convolution fusion | flops 3221225472 | bytes 12058624 | tf_op jit(solution)/shard_map/dot_general | solution.py:975
  294.1 11.4 %convolution_bitcast_fusion = f32[1,2048,1536]{2,1,0:T(8,128)} fusion(bf16[1024,1536]{1,0:T(8,128)(2,1)S(1)} %copy-done.8, bf16[1024,2176]{1,0:T(8,128)(2,1)} %bitcast.19.rows_ref), kind=kOutput, calls=%fused_computation | convolution fusion | flops 6442450944 | bytes 19922944 | tf_op jit(solution)/shard_map/dot_general | solution.py:975
  305.4 29.9 %all-to-all-done.2 = bf16[128,8,2176]{2,1,0:T(8,128)(2,1)} async-done(((bf16[128,8,2176]{2,1,0:T(8,128)(2,1)}), bf16[128,8,2176]{2,1,0:T(8,128)(2,1)}, u32[]{:S(2)}, u32[]{:S(2)}) %all-to-all-start.2) | async-done | bytes 4456480 | tf_op jit(solution)/shard_map/all_to_all | solution.py:1282
  335.4 28.2 %links_3.1 = (f32[128,2048]{1,0:T(8,128)}, f32[1,2048]{1,0:T(1,128)}, bf16[2048,128]{1,0:T(8,128)(2,1)}, bf16[2,4,128,2048]{3,2,1,0:T(8,128)(2,1)}) custom-call(bf16[1024,2176]{1,0:T(8,128)(2,1)} %bitcast.23.refs_0_, bf16[128,1024]{1,0:T(8,128)(2,1)} %get-tuple-element.70.refs_5_.refs_6_.refs_1_.refs_15_, f32[128,128]{1,0:T(8,128)} %get-tuple-element.88.refs_2_.refs_14_, ...), custom_call_target="tpu_custom_call" | custom-call | flops 24999999488 | bytes 75000000 | tf_op jit(solution)/shard_map/links_3/pallas_call | solution.py:117
  363.5 12.0 %all-to-all-start.3 = ((bf16[128,8,2048]{2,1,0:T(8,128)(2,1)}), bf16[128,8,2048]{2,1,0:T(8,128)(2,1)}, u32[]{:S(2)}, u32[]{:S(2)}) async-start(bf16[128,8,2048]{2,1,0:T(8,128)(2,1)} %bitcast.97), calls=%async_computation.3 | async-start | bytes 8388608 | tf_op jit(solution)/shard_map/all_to_all | solution.py:1282
  375.6 34.3 %attend_back.1 = (bf16[1024,512]{1,0:T(8,128)(2,1)}, f32[1,128]{1,0:T(1,128)}, bf16[64,256,128]{2,1,0:T(8,128)(2,1)}, bf16[64,256,128]{2,1,0:T(8,128)(2,1)}) custom-call(s32[4]{0:T(128)} %get-tuple-element.128.lo_ref, s32[4]{0:T(128)} %get-tuple-element.127.full_ref, s32[4]{0:T(128)} %copy-done.7, s32[64]{0:T(128)} %select_reduce_fusion.1.slot_ref, ...), custom_call_target="tpu_custom_call" | custom-call | flops 40000000000 | bytes 120000000 | tf_op jit(solution)/shard_map/attend_back/pallas_call | solution.py:1240
  410.6 43.2 %links_4.1 = (bf16[512,128]{1,0:T(8,128)(2,1)}, bf16[512,128]{1,0:T(8,128)(2,1)}, bf16[2048,512]{1,0:T(8,128)(2,1)}, bf16[2048,512]{1,0:T(8,128)(2,1)}) custom-call(bf16[2,4,4,512,128]{4,3,2,1,0:T(8,128)(2,1)} %bitcast.133, bf16[2,4,4,512,128]{4,3,2,1,0:T(8,128)(2,1)} %bitcast.134, bf16[1024,2048]{1,0:T(8,128)(2,1)} %bitcast.125, ...), custom_call_target="tpu_custom_call" | custom-call | flops 35000000512 | bytes 105000000 | tf_op jit(solution)/shard_map/links_4/pallas_call | solution.py:117
  453.8 62.2 %links_5.1 = (bf16[4,32,512]{2,1,0:T(8,128)(2,1)}, bf16[4,32,512]{2,1,0:T(8,128)(2,1)}, f32[40,128]{1,0:T(8,128)}, bf16[4,32,256]{2,1,0:T(8,128)(2,1)}, bf16[8,3...) custom-call(bf16[512,128]{1,0:T(8,128)(2,1)} %get-tuple-element.100.refs_0_, ...), custom_call_target="tpu_custom_call" | custom-call | flops 49999998976 | bytes 150000000 | tf_op jit(solution)/shard_map/links_5/pallas_call | solution.py:117
  516.1 1.3 slice_bitcast_fusion
  517.4 1.3 slice_bitcast_fusion.2
  518.6 0.9 convert_bitcast_fusion.1
  520.3 0.9 reshape.318
  522.6 0.9 convert_bitcast_fusion
  524.2 0.9 convert_reduce_fusion
  525.8 1.9 copy.68
  527.6 2.3 copy.69
  (58 shorter events, 11.5 us)
Async XLA Ops:
  0.6 193.2 %copy-start = (bf16[1,768,2048]{2,1,0:T(8,128)(2,1)S(1)}, bf16[1,768,2048]{2,1,0:T(8,128)(2,1)}, u32[]{:S(2)}) copy-start(bf16[1,768,2048]{2,1,0:T(8,128)(2,1)} %param.28) | copy-start | bytes 9437188
  2.4 66.0 %copy-start.7 = (s32[4]{0:T(128)}, s32[4]{0:T(128)S(1)}, u32[]{:S(2)}) copy-start(s32[4]{0:T(128)S(1)} %select_reduce_fusion.2.last_ref) | copy-start | bytes 52
  106.3 7.2 %copy-start.6 = (s32[64]{0:T(128)S(1)}, s32[64]{0:T(128)}, u32[]{:S(2)}) copy-start(s32[64]{0:T(128)} %param.30) | copy-start | bytes 772
  106.3 77.9 %all-to-all-start = ((bf16[128,8,2048]{2,1,0:T(8,128)(2,1)}), bf16[128,8,2048]{2,1,0:T(8,128)(2,1)}, u32[]{:S(2)}, u32[]{:S(2)}) async-start(bf16[128,8,2048]{2,1,0:T(8,128)(2,1)} %bitcast.98), calls=%async_computation | async-start | bytes 8388608 | tf_op jit(solution)/shard_map/all_to_all | solution.py:1282
  184.2 65.2 %all-to-all-start.1 = ((bf16[128,8,2176]{2,1,0:T(8,128)(2,1)}), bf16[128,8,2176]{2,1,0:T(8,128)(2,1)}, u32[]{:S(2)}, u32[]{:S(2)}) async-start(bf16[128,8,2176]{2,1,0:T(8,128)(2,1)} %bitcast.96), calls=%async_computation.1 | async-start | bytes 8912896 | tf_op jit(solution)/shard_map/all_to_all | solution.py:1282
  268.6 66.8 %all-to-all-start.2 = ((bf16[128,8,2176]{2,1,0:T(8,128)(2,1)}), bf16[128,8,2176]{2,1,0:T(8,128)(2,1)}, u32[]{:S(2)}, u32[]{:S(2)}) async-start(bf16[128,8,2176]{2,1,0:T(8,128)(2,1)} %bitcast.95), calls=%async_computation.2 | async-start | bytes 8912896 | tf_op jit(solution)/shard_map/all_to_all | solution.py:1282
  279.9 6.5 %copy-start.2 = (bf16[1024,768]{1,0:T(8,128)(2,1)S(1)}, bf16[1024,768]{1,0:T(8,128)(2,1)}, u32[]{:S(2)}) copy-start(bf16[1024,768]{1,0:T(8,128)(2,1)} %get-tuple-element.118) | copy-start | bytes 4718596
  286.4 7.7 %copy-start.8 = (bf16[1024,1536]{1,0:T(8,128)(2,1)S(1)}, bf16[1024,1536]{1,0:T(8,128)(2,1)}, u32[]{:S(2)}) copy-start(bf16[1024,1536]{1,0:T(8,128)(2,1)} %get-tuple-element.117) | copy-start | bytes 9437188
  363.5 90.3 %all-to-all-start.3 = ((bf16[128,8,2048]{2,1,0:T(8,128)(2,1)}), bf16[128,8,2048]{2,1,0:T(8,128)(2,1)}, u32[]{:S(2)}, u32[]{:S(2)}) async-start(bf16[128,8,2048]{2,1,0:T(8,128)(2,1)} %bitcast.97), calls=%async_computation.3 | async-start | bytes 8388608 | tf_op jit(solution)/shard_map/all_to_all | solution.py:1282
  375.6 34.3 %copy-start.4 = (f32[1,2048]{1,0:T(1,128)S(1)}, f32[1,2048]{1,0:T(1,128)}, u32[]{:S(2)}) copy-start(f32[1,2048]{1,0:T(1,128)} %get-tuple-element.105) | copy-start | bytes 24580
  375.6 35.0 %copy-start.3 = (f32[2048]{0:T(1024)S(1)}, f32[2048]{0:T(1024)}, u32[]{:S(2)}) copy-start(f32[2048]{0:T(1024)} %param.18) | copy-start | bytes 24580
  410.6 43.2 %copy-start.5 = (f32[10240]{0:T(1024)}, f32[10240]{0:T(1024)S(1)}, u32[]{:S(2)}) copy-start(f32[10240]{0:T(1024)S(1)} %constant_dynamic-update-slice_fusion) | copy-start | bytes 122884
  453.8 76.1 %copy-start.1 = (bf16[1,768,2048]{2,1,0:T(8,128)(2,1)S(1)}, bf16[1,768,2048]{2,1,0:T(8,128)(2,1)}, u32[]{:S(2)}) copy-start(bf16[1,768,2048]{2,1,0:T(8,128)(2,1)} %param.28) | copy-start | bytes 9437188
where the time goes:
time: 541 us; the launch traced here: 530 us
  Pallas kernels  350 us (65%)
  waiting for transfers between devices  78.2 us (14%)
  starting transfers between devices  39.7 us (7%)
  matrix products  32.9 us (6%)
  local copies, waits for them, and re-layouts  17.2 us (3%)
  other arithmetic  11.2 us (2%)
    pallas_call x6, Pallas kernels, launch(): pl.pallas_call(kernel, out_shape=tuple((jax.ShapeDtypeStruct(s, d) for f...  277 us
    all_to_all x4, waiting for transfers between devices, all_to_all(): lax.all_to_all(stacked, ('head', 'blk'), split_axis=0, concat_axis=0, til...  78.2 us
    all_to_all x4, starting transfers between devices, all_to_all(): lax.all_to_all(stacked, ('head', 'blk'), split_axis=0, concat_axis=0, til...  39.7 us
    pallas_call x1, Pallas kernels, attend_backward(): pl.pallas_call(attend_backward_kernel, out_shape=outs, grid_spec=pltpu.Pr...  34.3 us
    pallas_call x1, Pallas kernels, expert(): pl.pallas_call(expert_kernel, out_shape=outs, grid=(count // block,), in_...  19.2 us
    dot_general x2, matrix products, dot_tn(): lax.dot_general(a, b, (((0,), (0,)), ((), ())), preferred_element_type=F32)  19.1 us
    pallas_call x1, Pallas kernels, attend_forward(): pl.pallas_call(attend_forward_kernel, out_shape=outs, grid_spec=pltpu.Pre...  19 us
  transfers between devices with their start and end apart: 4, of which 2 were waited for; matrix products, arithmetic and copies ran while one was open for 7% of the time, Pallas kernels for 27%

commit v1 on v0

--- a/solution.py
+++ b/solution.py
@@ -1014,12 +1014,13 @@
 
 def key_tiles(lo, full, last, tiles):
     middle = jnp.minimum(full, last)
-    fours = lax.div(last - middle, 4)
+    twos, fours = lax.div(middle - lo, 2), lax.div(last - middle, 4)
     rest = middle + 4 * fours
-    pl.loop(lo, middle)(lambda t: tiles([t], True))
+    pl.loop(0, twos)(lambda i: tiles([lo + 2 * i, lo + 2 * i + 1], True))
+    pl.loop(lo + 2 * twos, middle)(lambda t: tiles([t], True))
     pl.loop(0, fours)(lambda i: tiles([middle + 4 * i + n for n in range(4)], False))
-    pl.loop(rest, last)(lambda t: tiles([t], False))
-    tiles([last], True)
+    for count in range(1, 5):
+        pl.when(last - rest == count - 1)(lambda count=count: tiles([rest + n for n in range(count)], True))
 
 
 def stacked(ref, slots):
@@ -1070,6 +1071,7 @@
     full_ref,
     last_ref,
     slot_ref,
+    block_ref,
     raw_ref,
     gain_ref,
     cos_ref,
@@ -1100,6 +1102,14 @@
 ):
     j = pl.program_id(0)
     slots, _, size = keys_ref.shape
+
+    def seen(s):
+        block = block_ref[s]
+        found = (block >= lo_ref[0]) & (block <= last_ref[0])
+        for i in range(1, lo_ref.shape[0]):
+            found |= (block >= lo_ref[i]) & (block <= last_ref[i])
+        return found
+
     takes = [pltpu.make_async_copy(k_ref, keys_ref, local.at[0]), pltpu.make_async_copy(v_ref, values_ref, local.at[1])]
     heads = raw_ref.shape[1] // size
     scale = size**-0.5
@@ -1113,8 +1123,10 @@
 
         @pl.loop(0, slots)
         def _(s):
-            dk[s] = jnp.zeros(dk.shape[1:], F32)
-            dv[s] = jnp.zeros(dv.shape[1:], F32)
+            @pl.when(seen(s))
+            def _():
+                dk[s] = jnp.zeros(dk.shape[1:], F32)
+                dv[s] = jnp.zeros(dv.shape[1:], F32)
 
     attended_grad = dot_nn(g_ref[...], w_ref[...]).astype(BF)
     for n in range(heads):
@@ -1166,9 +1178,18 @@
 
         @pl.loop(0, slots, step=8)
         def _(s):
-            for i in range(8):
-                keys_ref[s + i] = (dk[s + i] * scale).astype(BF)
-                values_ref[s + i] = dv[s + i].astype(BF)
+            @pl.loop(s, s + 8)
+            def _(i):
+                @pl.when(seen(i))
+                def _():
+                    keys_ref[i] = (dk[i] * scale).astype(BF)
+                    values_ref[i] = dv[i].astype(BF)
+
+                @pl.when(jnp.logical_not(seen(i)))
+                def _():
+                    keys_ref[i] = jnp.zeros(keys_ref.shape[1:], BF)
+                    values_ref[i] = jnp.zeros(values_ref.shape[1:], BF)
+
             for copy in out(s, 8):
                 copy.start()
 
@@ -1241,7 +1262,7 @@
         attend_backward_kernel,
         out_shape=outs,
         grid_spec=pltpu.PrefetchScalarGridSpec(
-            num_scalar_prefetch=4,
+            num_scalar_prefetch=5,
             grid=(blocks,),
             in_specs=[
                 by_rows(raw),
@@ -1398,8 +1419,9 @@
     grad_group = grad_group.reshape(group_rows, width)
     grad_group, expert_out = lax.optimization_barrier((grad_group, expert_out))
     expert_out = all_to_all(expert_out.reshape(devices, cap, width)).reshape(-1, width)
+    block_of = block_deal.reshape(-1, 2, 2).transpose(2, 0, 1).reshape(-1)
     grad_q, grad_query_gain, grad_keys, grad_values = attend_backward(
-        meta, q_raw, q_gain, cosine, sine, keys, values, start_rows, queries, attended, grad_group, w_out_t, logs
+        (*meta, block_of), q_raw, q_gain, cosine, sine, keys, values, start_rows, queries, attended, grad_group, w_out_t, logs
     )
 
     split = (2, 4, 4, group_rows // 2, size)

time: 541 us -> 543 us (level)
  transfers between devices with their start and end apart: 4 -> 4, of which waited for: 2 -> 2; matrix products, arithmetic and copies ran while one was open for 7% -> 7% of each run, Pallas kernels for 27% -> 28%
where the time goes in v1:
time: 543 us; the launch traced here: 536 us
  Pallas kernels  355 us (65%)
  waiting for transfers between devices  77.2 us (14%)
  starting transfers between devices  39.4 us (7%)
  matrix products  32.8 us (6%)
  local copies, waits for them, and re-layouts  18.2 us (3%)
  other arithmetic  11.2 us (2%)
    pallas_call x6, Pallas kernels, launch(): pl.pallas_call(kernel, out_shape=tuple((jax.ShapeDtypeStruct(s, d) for f...  282 us
    all_to_all x4, waiting for transfers between devices, all_to_all(): lax.all_to_all(stacked, ('head', 'blk'), split_axis=0, concat_axis=0, til...  77.2 us
    all_to_all x4, starting transfers between devices, all_to_all(): lax.all_to_all(stacked, ('head', 'blk'), split_axis=0, concat_axis=0, til...  39.4 us
    pallas_call x1, Pallas kernels, attend_backward(): pl.pallas_call(attend_backward_kernel, out_shape=outs, grid_spec=pltpu.Pr...  35.8 us
    pallas_call x1, Pallas kernels, expert(): pl.pallas_call(expert_kernel, out_shape=outs, grid=(count // block,), in_...  19.2 us
    dot_general x2, matrix products, dot_tn(): lax.dot_general(a, b, (((0,), (0,)), ((), ())), preferred_element_type=F32)  19 us
    pallas_call x1, Pallas kernels, attend_forward(): pl.pallas_call(attend_forward_kernel, out_shape=outs, grid_spec=pltpu.Pre...  17.9 us
  transfers between devices with their start and end apart: 4, of which 2 were waited for; matrix products, arithmetic and copies ran while one was open for 7% of the time, Pallas kernels for 28%

profile of v1, /device:TPU:1, one launch (start us, length us, event | category | flops | bytes accessed | tf_op | source)
XLA Modules:
  0.0 535.5 jit_solution(14312622757107588032)
XLA Ops:
  0.7 0.8 broadcast_add_fusion
  1.5 0.9 select_reduce_fusion.2.last_ref
  3.4 1.0 reshape.291
  6.1 1.4 copy.52.refs_7_
  10.1 58.4 %links_0.1 = (bf16[4,4,4,32,768]{4,3,2,1,0:T(8,128)(2,1)}, bf16[4,4,4,32,512]{4,3,2,1,0:T(8,128)(2,1)}, bf16[4,4,8,32,128]{4,3,2,1,0:T(8,128)(2,1)}, bf16[2,4,12...) custom-call(bf16[128,2048]{1,0:T(8,128)(2,1)} %refs_17_.1, ...), custom_call_target="tpu_custom_call" | custom-call | flops 44999999488 | bytes 135000000 | tf_op jit(solution)/shard_map/links_0/pallas_call | solution.py:117
  68.5 37.8 %links_1.1 = (f32[1024,512]{1,0:T(8,128)}, f32[512,128]{1,0:T(8,128)}, bf16[2,4,4,512,128]{4,3,2,1,0:T(8,128)(2,1)}, bf16[2,4,4,512,128]{4,3,2,1,0:T(8,128)(2,1)}, bf16[1024,2048]{1,0:T(8,128)(2,1)}) custom-call(bf16[1024,2048]{1,0:T(8,128)(2,1)} %bitcast.126, bf16[2048,768]{1,0:T(8,128)(2,1)} %bitcast.137, f32[1,128]{1,0:T(1,128)} %bitcast.124, ...), custom_call_target="tpu_custom_call" | custom-call | flops 35000000512 | bytes 105000000 | tf_op jit(solution)/shard_map/links_1/pallas_call | solution.py:117
  106.3 6.8 %all-to-all-start = ((bf16[128,8,2048]{2,1,0:T(8,128)(2,1)}), bf16[128,8,2048]{2,1,0:T(8,128)(2,1)}, u32[]{:S(2)}, u32[]{:S(2)}) async-start(bf16[128,8,2048]{2,1,0:T(8,128)(2,1)} %bitcast.99), calls=%async_computation | async-start | bytes 8388608 | tf_op jit(solution)/shard_map/all_to_all | solution.py:1303
  115.2 17.9 %attend.1 = (bf16[1024,512]{1,0:T(8,128)(2,1)}, bf16[1024,512]{1,0:T(8,128)(2,1)}, f32[4,1,1024]{2,1,0:T(1,128)}) custom-call(s32[4]{0:T(128)} %get-tuple-element.128.lo_ref, s32[4]{0:T(128)} %get-tuple-element.127.full_ref, s32[4]{0:T(128)} %copy-done.7, s32[64]{0:T(128)} %select_reduce_fusion.1.slot_ref, f32[1024,512]{1,0:T(8,128)} %get-tuple-element.71.raw_ref, ...), custom_call_target="tpu_custom_call" | custom-call | flops 30000001024 | bytes 90000000 | tf_op jit(solution)/shard_map/attend/pallas_call | solution.py:1232
  133.2 2.3 reduce_sum.60
  135.5 48.6 %links_2.1 = (f32[128,2048]{1,0:T(8,128)}, bf16[128,2048]{1,0:T(8,128)(2,1)}, f32[128,128]{1,0:T(8,128)}, bf16[1024,2176]{1,0:T(8,128)(2,1)}) custom-call(bf16[1024,512]{1,0:T(8,128)(2,1)} %get-tuple-element.75.refs_0_.o_ref.refs_5_, bf16[2048,512]{1,0:T(8,128)(2,1)} %bitcast.139, bf16[128,2048]{1,0:T(8,128)(2,1)} %refs_17_.1, f32[1,2048]{1,0:T(1,128)} %bitcast.120, ...), custom_call_target="tpu_custom_call" | custom-call | flops 30000001024 | bytes 90000000 | tf_op jit(solution)/shard_map/links_2/pallas_call | solution.py:117
  184.1 9.5 %all-to-all-start.1 = ((bf16[128,8,2176]{2,1,0:T(8,128)(2,1)}), bf16[128,8,2176]{2,1,0:T(8,128)(2,1)}, u32[]{:S(2)}, u32[]{:S(2)}) async-start(bf16[128,8,2176]{2,1,0:T(8,128)(2,1)} %bitcast.97), calls=%async_computation.1 | async-start | bytes 8912896 | tf_op jit(solution)/shard_map/all_to_all | solution.py:1303
  193.6 7.3 %fusion.2.plain_ref = f32[1024,768]{1,0:T(8,128)} fusion(bf16[1024,2048]{1,0:T(8,128)(2,1)} %bitcast.18, bf16[1,768,2048]{2,1,0:T(8,128)(2,1)S(1)} %copy-done), kind=kOutput, calls=%fused_computation.5 | convolution fusion | flops 3221225472 | bytes 10485760 | tf_op jit(solution)/shard_map/dot_general | solution.py:971
  200.9 48.2 %all-to-all-done.1 = bf16[128,8,2176]{2,1,0:T(8,128)(2,1)} async-done(((bf16[128,8,2176]{2,1,0:T(8,128)(2,1)}), bf16[128,8,2176]{2,1,0:T(8,128)(2,1)}, u32[]{:S(2)}, u32[]{:S(2)}) %all-to-all-start.1) | async-done | bytes 4456480 | tf_op jit(solution)/shard_map/all_to_all | solution.py:1303
  249.1 19.2 %expert.1 = (bf16[1024,2176]{1,0:T(8,128)(2,1)}, bf16[1024,768]{1,0:T(8,128)(2,1)}, bf16[1024,768]{1,0:T(8,128)(2,1)}, bf16[1024,1536]{1,0:T(8,128)(2,1)}) custom-call(bf16[1024,2176]{1,0:T(8,128)(2,1)} %bitcast.20.rows_ref, f32[1024,768]{1,0:T(8,128)} %fusion.2.plain_ref, bf16[2048,1536]{1,0:T(8,128)(2,1)} %bitcast.119), custom_call_target="tpu_custom_call" | custom-call | flops 20000000000 | bytes 60000000 | tf_op jit(solution)/shard_map/expert/pallas_call | solution.py:1215
  268.4 11.6 %all-to-all-start.2 = ((bf16[128,8,2176]{2,1,0:T(8,128)(2,1)}), bf16[128,8,2176]{2,1,0:T(8,128)(2,1)}, u32[]{:S(2)}, u32[]{:S(2)}) async-start(bf16[128,8,2176]{2,1,0:T(8,128)(2,1)} %bitcast.96), calls=%async_computation.2 | async-start | bytes 8912896 | tf_op jit(solution)/shard_map/all_to_all | solution.py:1303
  280.9 6.5 %convolution_convert_fusion = bf16[1024,2048]{1,0:T(8,128)(2,1)} fusion(bf16[1024,768]{1,0:T(8,128)(2,1)} %get-tuple-element.86, bf16[1,768,2048]{2,1,0:T(8,128)(2,1)S(1)} %copy-done), kind=kOutput, calls=%fused_computation.3 | convolution fusion | flops 3223322624 | bytes 8912896 | tf_op jit(solution)/shard_map/dot_general | solution.py:967
  287.4 7.7 %convolution_bitcast_fusion.1 = f32[1,768,2048]{2,1,0:T(8,128)} fusion(bf16[1024,768]{1,0:T(8,128)(2,1)S(1)} %copy-done.2, bf16[1024,2048]{1,0:T(8,128)(2,1)} %bitcast.18), kind=kOutput, calls=%fused_computation.2 | convolution fusion | flops 3221225472 | bytes 12058624 | tf_op jit(solution)/shard_map/dot_general | solution.py:975
  295.1 11.4 %convolution_bitcast_fusion = f32[1,2048,1536]{2,1,0:T(8,128)} fusion(bf16[1024,1536]{1,0:T(8,128)(2,1)S(1)} %copy-done.8, bf16[1024,2176]{1,0:T(8,128)(2,1)} %bitcast.20.rows_ref), kind=kOutput, calls=%fused_computation | convolution fusion | flops 6442450944 | bytes 19922944 | tf_op jit(solution)/shard_map/dot_general | solution.py:975
  306.5 29.0 %all-to-all-done.2 = bf16[128,8,2176]{2,1,0:T(8,128)(2,1)} async-done(((bf16[128,8,2176]{2,1,0:T(8,128)(2,1)}), bf16[128,8,2176]{2,1,0:T(8,128)(2,1)}, u32[]{:S(2)}, u32[]{:S(2)}) %all-to-all-start.2) | async-done | bytes 4456480 | tf_op jit(solution)/shard_map/all_to_all | solution.py:1303
  335.5 28.2 %links_3.1 = (f32[128,2048]{1,0:T(8,128)}, f32[1,2048]{1,0:T(1,128)}, bf16[2048,128]{1,0:T(8,128)(2,1)}, bf16[2,4,128,2048]{3,2,1,0:T(8,128)(2,1)}) custom-call(bf16[1024,2176]{1,0:T(8,128)(2,1)} %bitcast.24.refs_0_, bf16[128,1024]{1,0:T(8,128)(2,1)} %get-tuple-element.70.refs_5_.refs_6_.refs_1_.refs_15_, f32[128,128]{1,0:T(8,128)} %get-tuple-element.88.refs_2_.refs_14_, ...), custom_call_target="tpu_custom_call" | custom-call | flops 24999999488 | bytes 75000000 | tf_op jit(solution)/shard_map/links_3/pallas_call | solution.py:117
  363.6 11.6 %all-to-all-start.3 = ((bf16[128,8,2048]{2,1,0:T(8,128)(2,1)}), bf16[128,8,2048]{2,1,0:T(8,128)(2,1)}, u32[]{:S(2)}, u32[]{:S(2)}) async-start(bf16[128,8,2048]{2,1,0:T(8,128)(2,1)} %bitcast.98), calls=%async_computation.3 | async-start | bytes 8388608 | tf_op jit(solution)/shard_map/all_to_all | solution.py:1303
  375.3 35.8 %attend_back.1 = (bf16[1024,512]{1,0:T(8,128)(2,1)}, f32[1,128]{1,0:T(1,128)}, bf16[64,256,128]{2,1,0:T(8,128)(2,1)}, bf16[64,256,128]{2,1,0:T(8,128)(2,1)}) custom-call(s32[4]{0:T(128)} %get-tuple-element.128.lo_ref, s32[4]{0:T(128)} %get-tuple-element.127.full_ref, s32[4]{0:T(128)} %copy-done.7, s32[64]{0:T(128)} %select_reduce_fusion.1.slot_ref, ...), custom_call_target="tpu_custom_call" | custom-call | flops 40000000000 | bytes 120000000 | tf_op jit(solution)/shard_map/attend_back/pallas_call | solution.py:1261
  411.9 46.8 %links_4.1 = (bf16[512,128]{1,0:T(8,128)(2,1)}, bf16[512,128]{1,0:T(8,128)(2,1)}, bf16[2048,512]{1,0:T(8,128)(2,1)}, bf16[2048,512]{1,0:T(8,128)(2,1)}) custom-call(bf16[2,4,4,512,128]{4,3,2,1,0:T(8,128)(2,1)} %bitcast.135, bf16[2,4,4,512,128]{4,3,2,1,0:T(8,128)(2,1)} %bitcast.136, bf16[1024,2048]{1,0:T(8,128)(2,1)} %bitcast.127, ...), custom_call_target="tpu_custom_call" | custom-call | flops 35000000512 | bytes 105000000 | tf_op jit(solution)/shard_map/links_4/pallas_call | solution.py:117
  458.7 62.5 %links_5.1 = (bf16[4,32,512]{2,1,0:T(8,128)(2,1)}, bf16[4,32,512]{2,1,0:T(8,128)(2,1)}, f32[40,128]{1,0:T(8,128)}, bf16[4,32,256]{2,1,0:T(8,128)(2,1)}, bf16[8,3...) custom-call(bf16[512,128]{1,0:T(8,128)(2,1)} %get-tuple-element.100.refs_0_, ...), custom_call_target="tpu_custom_call" | custom-call | flops 49999998976 | bytes 150000000 | tf_op jit(solution)/shard_map/links_5/pallas_call | solution.py:117
  521.2 1.3 slice_bitcast_fusion
  522.5 1.3 slice_bitcast_fusion.2
  523.8 0.9 convert_bitcast_fusion.1
  525.5 0.9 reshape.326
  527.7 0.9 convert_bitcast_fusion
  529.4 0.9 convert_reduce_fusion
  530.9 1.9 copy.73
  532.8 2.3 copy.74
  (61 shorter events, 12.5 us)
Async XLA Ops:
  0.6 193.0 %copy-start = (bf16[1,768,2048]{2,1,0:T(8,128)(2,1)S(1)}, bf16[1,768,2048]{2,1,0:T(8,128)(2,1)}, u32[]{:S(2)}) copy-start(bf16[1,768,2048]{2,1,0:T(8,128)(2,1)} %param.28) | copy-start | bytes 9437188
  2.4 66.0 %copy-start.7 = (s32[4]{0:T(128)}, s32[4]{0:T(128)S(1)}, u32[]{:S(2)}) copy-start(s32[4]{0:T(128)S(1)} %select_reduce_fusion.2.last_ref) | copy-start | bytes 52
  106.3 7.1 %copy-start.6 = (s32[64]{0:T(128)S(1)}, s32[64]{0:T(128)}, u32[]{:S(2)}) copy-start(s32[64]{0:T(128)} %param.30) | copy-start | bytes 772
  106.3 77.8 %all-to-all-start = ((bf16[128,8,2048]{2,1,0:T(8,128)(2,1)}), bf16[128,8,2048]{2,1,0:T(8,128)(2,1)}, u32[]{:S(2)}, u32[]{:S(2)}) async-start(bf16[128,8,2048]{2,1,0:T(8,128)(2,1)} %bitcast.99), calls=%async_computation | async-start | bytes 8388608 | tf_op jit(solution)/shard_map/all_to_all | solution.py:1303
  184.1 65.0 %all-to-all-start.1 = ((bf16[128,8,2176]{2,1,0:T(8,128)(2,1)}), bf16[128,8,2176]{2,1,0:T(8,128)(2,1)}, u32[]{:S(2)}, u32[]{:S(2)}) async-start(bf16[128,8,2176]{2,1,0:T(8,128)(2,1)} %bitcast.97), calls=%async_computation.1 | async-start | bytes 8912896 | tf_op jit(solution)/shard_map/all_to_all | solution.py:1303
  268.4 67.1 %all-to-all-start.2 = ((bf16[128,8,2176]{2,1,0:T(8,128)(2,1)}), bf16[128,8,2176]{2,1,0:T(8,128)(2,1)}, u32[]{:S(2)}, u32[]{:S(2)}) async-start(bf16[128,8,2176]{2,1,0:T(8,128)(2,1)} %bitcast.96), calls=%async_computation.2 | async-start | bytes 8912896 | tf_op jit(solution)/shard_map/all_to_all | solution.py:1303
  280.9 6.5 %copy-start.2 = (bf16[1024,768]{1,0:T(8,128)(2,1)S(1)}, bf16[1024,768]{1,0:T(8,128)(2,1)}, u32[]{:S(2)}) copy-start(bf16[1024,768]{1,0:T(8,128)(2,1)} %get-tuple-element.118) | copy-start | bytes 4718596
  287.4 7.7 %copy-start.8 = (bf16[1024,1536]{1,0:T(8,128)(2,1)S(1)}, bf16[1024,1536]{1,0:T(8,128)(2,1)}, u32[]{:S(2)}) copy-start(bf16[1024,1536]{1,0:T(8,128)(2,1)} %get-tuple-element.117) | copy-start | bytes 9437188
  363.6 95.1 %all-to-all-start.3 = ((bf16[128,8,2048]{2,1,0:T(8,128)(2,1)}), bf16[128,8,2048]{2,1,0:T(8,128)(2,1)}, u32[]{:S(2)}, u32[]{:S(2)}) async-start(bf16[128,8,2048]{2,1,0:T(8,128)(2,1)} %bitcast.98), calls=%async_computation.3 | async-start | bytes 8388608 | tf_op jit(solution)/shard_map/all_to_all | solution.py:1303
  375.3 35.8 %copy-start.4 = (f32[1,2048]{1,0:T(1,128)S(1)}, f32[1,2048]{1,0:T(1,128)}, u32[]{:S(2)}) copy-start(f32[1,2048]{1,0:T(1,128)} %get-tuple-element.105) | copy-start | bytes 24580
  375.3 36.5 %copy-start.3 = (f32[2048]{0:T(1024)S(1)}, f32[2048]{0:T(1024)}, u32[]{:S(2)}) copy-start(f32[2048]{0:T(1024)} %param.18) | copy-start | bytes 24580
  411.8 46.9 %copy-start.5 = (f32[10240]{0:T(1024)}, f32[10240]{0:T(1024)S(1)}, u32[]{:S(2)}) copy-start(f32[10240]{0:T(1024)S(1)} %constant_dynamic-update-slice_fusion) | copy-start | bytes 122884
  458.7 76.4 %copy-start.1 = (bf16[1,768,2048]{2,1,0:T(8,128)(2,1)S(1)}, bf16[1,768,2048]{2,1,0:T(8,128)(2,1)}, u32[]{:S(2)}) copy-start(bf16[1,768,2048]{2,1,0:T(8,128)(2,1)} %param.28) | copy-start | bytes 9437188

commit v2 on v1

--- a/solution.py
+++ b/solution.py
@@ -401,6 +401,39 @@
     )
 
 
+def ring_exchange_flow(array, columns, kind):
+    n, rows = SIZES[kind], array.shape[0]
+
+    def steps(ins, outs, scratch):
+        (src,), (out,) = ins, outs
+        send, recv, local = scratch
+        mine, at = peers_of(kind)
+
+        def part(to):
+            return src if kind == "z" else src.at[:, pl.ds(pl.multiple_of(to * columns, columns), columns)]
+
+        own = pltpu.make_async_copy(part(mine), out.at[mine], local.at[0])
+        own.start()
+        yield
+        copies = []
+        for k in range(1, n):
+            to = lax.rem(mine + k, n)
+            copies.append(remote(part(to), out.at[mine], send.at[k], recv.at[k], at(to)))
+            copies[-1].start()
+        yield 40.0
+        own.wait()
+        for copy in copies:
+            copy.wait()
+
+    return Flow(
+        [(array, pl.ANY)],
+        [((n, rows, columns), BF, pltpu.VMEM)],
+        [dma(n), dma(n), dma(1)],
+        [(kind, k) for k in range(1, n)],
+        steps,
+    )
+
+
 def product_flow(left, right):
     columns, width = left.shape[1], right.shape[1]
 
@@ -496,7 +529,7 @@
     out[...] = jnp.sum(far[...], axis=0) / gains[1]
 
 
-def product_scatter_flow(lefts, right, done, units=None, gains=None, key_gain=None):
+def product_scatter_flow(lefts, right, done, units=None, gains=None, key_gain=None, kept=None):
     arrays = [left for left in lefts if not isinstance(left, Made)]
     own, wide = lefts[0].shape[0] // 8, right.shape[0]
     spans = [0]
@@ -507,6 +540,8 @@
         given = list(ins[: len(arrays)])
         left_refs = [left.ref if isinstance(left, Made) else given.pop(0) for left in lefts]
         right_ref = ins[len(arrays)]
+        if kept is not None:
+            kept.ref = right_ref
         out, theirs, came, chunks, bufs, send, recv, pass_send, pass_recv, *rest = scratch
         core, member = peers_of("c")
         me, _ = peers_of("zc")
@@ -826,12 +861,12 @@
     )
 
 
-def route_flow(tokens, gain, router, chosen, assign, done):
+def route_flow(tokens, gain, weights, chosen, assign, done):
     own, width = tokens.shape
     experts, count = chosen.shape[1], assign.shape[1]
 
     def steps(ins, outs, scratch):
-        tokens_ref, gain_ref, router_ref, chosen_ref, assign_ref = ins
+        tokens_ref, gain_ref, chosen_ref, assign_ref = ins
         residual_ref, mixed_ref, gates_ref, rows_ref = outs
         (pick,) = scratch
         yield
@@ -840,7 +875,7 @@
         residual = tokens_ref[...].astype(F32) + done.ref[...]
         residual_ref[...] = residual
         mixed_ref[...] = (residual * lax.rsqrt(jnp.mean(residual * residual, axis=-1, keepdims=True) + EPS) * gain_ref[...]).astype(BF)
-        logits = jnp.where(chosen_ref[...] > 0, dot_nn(mixed_ref[...], router_ref[...]), -1e30)
+        logits = jnp.where(chosen_ref[...] > 0, dot_nn(mixed_ref[...], weights.ref[:, -experts:]), -1e30)
         powers = jnp.exp(logits - jnp.max(logits, axis=-1, keepdims=True))
         gates = powers / jnp.sum(powers, axis=-1, keepdims=True)
         gates_ref[...] = gates
@@ -851,7 +886,7 @@
         yield
 
     return Flow(
-        [(x, pltpu.VMEM) for x in (tokens, gain, router, chosen, assign)],
+        [(x, pltpu.VMEM) for x in (tokens, gain, chosen, assign)],
         [
             ((own, width), F32, pltpu.VMEM),
             ((own, width), BF, pltpu.VMEM),
@@ -864,17 +899,23 @@
     )
 
 
-def mix_back_flow(back, assign, gates, mixed, router, residual, gain, cotangent, made):
+def mix_back_flow(back, assign, gates, mixed, weights, residual, gain, cotangent, made):
     own, width = mixed.shape
     experts, count = gates.shape[1], back.shape[0]
 
     def steps(ins, outs, scratch):
-        back_hbm, assign_ref, gates_ref, mixed_ref, router_ref, residual_ref, gain_ref, cotangent_ref = ins
+        back_hbm, weights_hbm, assign_ref, gates_ref, mixed_ref, residual_ref, gain_ref, cotangent_ref = ins
         residual_grad, gain_grad, router_grad = outs
-        back_ref, mixed_grad, made.ref, local = scratch
-        copy = pltpu.make_async_copy(back_hbm, back_ref, local.at[0])
-        copy.start()
-        copy.wait()
+        back_ref, mixed_grad, made.ref, router_ref, local = scratch
+        last = pl.ds(weights_hbm.shape[1] - experts, experts)
+        copies = [
+            pltpu.make_async_copy(back_hbm, back_ref, local.at[0]),
+            pltpu.make_async_copy(weights_hbm.at[:, last], router_ref, local.at[1]),
+        ]
+        for copy in copies:
+            copy.start()
+        for copy in copies:
+            copy.wait()
         sums = jnp.sum(back_ref[:, width : width + 128].astype(F32), axis=1, keepdims=True)
         shape = (count, experts)
         expert_of = lax.div(lax.broadcasted_iota(jnp.int32, shape, 0), count // experts)
@@ -902,9 +943,15 @@
         yield
 
     return Flow(
-        [(back, pl.ANY)] + [(x, pltpu.VMEM) for x in (assign, gates, mixed, router, residual, gain, cotangent)],
+        [(back, pl.ANY), (weights, pl.ANY)] + [(x, pltpu.VMEM) for x in (assign, gates, mixed, residual, gain, cotangent)],
         [((own, width), F32, pltpu.VMEM), ((1, width), F32, pltpu.VMEM), ((width, experts), BF, pltpu.VMEM)],
-        [pltpu.VMEM(back.shape, BF), pltpu.VMEM((own, width), F32), pltpu.VMEM((own, width), BF), dma(1)],
+        [
+            pltpu.VMEM(back.shape, BF),
+            pltpu.VMEM((own, width), F32),
+            pltpu.VMEM((own, width), BF),
+            pltpu.VMEM((width, experts), BF),
+            dma(2),
+        ],
         [],
         steps,
     )
@@ -1275,7 +1322,7 @@
                 by_rows(queries),
                 by_rows(attended),
                 by_rows(grads),
-                resident(w_out_t),
+                pl.BlockSpec((w_out_t.shape[0], wide), lambda j, *_: (0, 0), pipeline_mode=pl.Buffered(1)),
                 by_rows(logs, 1),
             ],
             out_specs=(by_rows(outs[0]), resident(outs[1])) + (pl.BlockSpec(memory_space=pl.ANY),) * 2,
@@ -1355,12 +1402,12 @@
     out_pack = w_out.reshape(4, q_cols, depth).transpose(2, 0, 1).reshape(depth, -1)
     side = lax.axis_index("head") == jnp.arange(2, dtype=jnp.int32)
     router_pack = jnp.where(side[None, :, None], w_router.T[:, None, :], 0).astype(BF).reshape(depth, experts)
-    w_qkv, w_out_t, w_router_t, group_tokens, assign_low, chosen, cosine, sine = launch(
+    w_qkv, out_part, router_part, group_tokens, assign_low, chosen, cosine, sine = launch(
         [
             norm_flow(tokens, norm_gain[None], normed),
             plane_gather_flow([(w_query, q_cols, 1), (key_weight, size, 2), (value_weight, size, 2)], "x", "y", ahead="zhc"),
-            plane_gather_flow([(out_pack, q_cols, 1)], "y", "x", ahead="zhc"),
-            plane_gather_flow([(router_pack, experts, 1)], "y", "x", ahead="z"),
+            ring_exchange_flow(out_pack, q_cols, "zhc"),
+            ring_exchange_flow(router_pack, experts, "z"),
             ring_gather_flow(normed),
             tables_flow(routes, offsets, spacing, experts, cap),
         ],
@@ -1368,8 +1415,11 @@
         45,
     )
     normed_group = group_tokens.reshape(group_rows, width)
-    w_qkv, w_out_t = w_qkv.reshape(width, -1), w_out_t.reshape(width, -1)
-    w_router_t = jnp.sum(w_router_t.reshape(-1, 2, depth, experts), axis=1).reshape(width, experts)
+    w_qkv = w_qkv.reshape(width, -1)
+    router_part = jnp.sum(router_part.reshape(4, 2, depth, experts), axis=1)
+    w_rest = jnp.concatenate([out_part, router_part], axis=2).reshape(4 * depth, -1)
+    planes = [[j * 4 + r for j in range(16)] for r in range(4)]
+    w_rest = lax.all_gather(w_rest, "blk", axis_index_groups=planes, axis=0, tiled=True)
 
     q_gain, k_gain = query_gain[None], key_gain[None]
     key, value = Made(group_rows // 2, size), Made(group_rows // 2, size)
@@ -1387,11 +1437,11 @@
     keys, values = keys.reshape(-1, BLOCK, size), values.reshape(-1, BLOCK, size)
     queries, attended, logs = attend_forward(meta, q_raw, q_gain, cosine, sine, keys, values, start_rows)
 
-    attention = Made(own, width)
+    attention, weights_kept = Made(own, width), Made()
     residual, mixed, gates, outgoing = launch(
         [
-            product_scatter_flow([attended], w_out_t, attention),
-            route_flow(tokens, mix_gain[None], w_router_t, chosen, assign_low, attention),
+            product_scatter_flow([attended], w_rest, attention, kept=weights_kept),
+            route_flow(tokens, mix_gain[None], weights_kept, chosen, assign_low, attention),
         ],
         2,
         30,
@@ -1410,7 +1460,7 @@
     grad_attention = Made(own, width)
     grad_residual, grad_mix_gain, grad_router_t, grad_group = launch(
         [
-            mix_back_flow(back, assign_low, gates, mixed, w_router_t, residual, mix_gain[None], cotangent, grad_attention),
+            mix_back_flow(back, assign_low, gates, mixed, w_rest, residual, mix_gain[None], cotangent, grad_attention),
             ring_gather_flow(grad_attention),
         ],
         3,
@@ -1421,7 +1471,7 @@
     expert_out = all_to_all(expert_out.reshape(devices, cap, width)).reshape(-1, width)
     block_of = block_deal.reshape(-1, 2, 2).transpose(2, 0, 1).reshape(-1)
     grad_q, grad_query_gain, grad_keys, grad_values = attend_backward(
-        (*meta, block_of), q_raw, q_gain, cosine, sine, keys, values, start_rows, queries, attended, grad_group, w_out_t, logs
+        (*meta, block_of), q_raw, q_gain, cosine, sine, keys, values, start_rows, queries, attended, grad_group, w_rest, logs
     )
 
     split = (2, 4, 4, group_rows // 2, size)

time: 543 us -> 554 us (1.020)
  between operations: 1.43 us -> 14.8 us
  transfers between devices with their start and end apart: 4 -> 5, of which waited for: 2 -> 2; matrix products, arithmetic and copies ran while one was open for 7% -> 7% of each run, Pallas kernels for 28% -> 35%
where the time goes in v2:
time: 554 us; the launch traced here: 547 us
  Pallas kernels  353 us (64%)
  waiting for transfers between devices  77.3 us (14%)
  starting transfers between devices  39.6 us (7%)
  matrix products  32.9 us (6%)
  local copies, waits for them, and re-layouts  18.2 us (3%)
  between operations  14.8 us (3%)
  other arithmetic  11.2 us (2%)
    pallas_call x6, Pallas kernels, launch(): pl.pallas_call(kernel, out_shape=tuple((jax.ShapeDtypeStruct(s, d) for f...  279 us
    all_to_all x4, waiting for transfers between devices, all_to_all(): lax.all_to_all(stacked, ('head', 'blk'), split_axis=0, concat_axis=0, til...  77.2 us
    all_to_all x4, starting transfers between devices, all_to_all(): lax.all_to_all(stacked, ('head', 'blk'), split_axis=0, concat_axis=0, til...  39.6 us
    pallas_call x1, Pallas kernels, attend_backward(): pl.pallas_call(attend_backward_kernel, out_shape=outs, grid_spec=pltpu.Pr...  36.7 us
    pallas_call x1, Pallas kernels, expert(): pl.pallas_call(expert_kernel, out_shape=outs, grid=(count // block,), in_...  19.2 us
    dot_general x2, matrix products, dot_tn(): lax.dot_general(a, b, (((0,), (0,)), ((), ())), preferred_element_type=F32)  19.1 us
    pallas_call x1, Pallas kernels, attend_forward(): pl.pallas_call(attend_forward_kernel, out_shape=outs, grid_spec=pltpu.Pre...  18.5 us
  transfers between devices with their start and end apart: 5, of which 2 were waited for; matrix products, arithmetic and copies ran while one was open for 7% of the time, Pallas kernels for 35%

profile of v2, /device:TPU:1, one launch (start us, length us, event | category | flops | bytes accessed | tf_op | source)
XLA Modules:
  0.0 547.4 jit_solution(3356152778030592909)
XLA Ops:
  8.1 0.9 select_reduce_fusion.2.last_ref
  10.0 1.0 reshape.288
  12.6 1.4 copy.52.refs_7_
  16.6 50.4 %links_0.1 = (bf16[4,4,4,32,768]{4,3,2,1,0:T(8,128)(2,1)}, bf16[4,32,512]{2,1,0:T(8,128)(2,1)}, bf16[8,32,128]{2,1,0:T(8,128)(2,1)}, bf16[2,4,128,2048]{3,2,1,0:...) custom-call(bf16[128,2048]{1,0:T(8,128)(2,1)} %refs_17_.1, ...), custom_call_target="tpu_custom_call" | custom-call | flops 44999999488 | bytes 135000000 | tf_op jit(solution)/shard_map/links_0/pallas_call | solution.py:117
  67.0 0.9 bitcast_reduce_fusion
  67.9 1.6 pad_maximum_fusion
  69.5 38.2 %links_1.1 = (f32[1024,512]{1,0:T(8,128)}, f32[512,128]{1,0:T(8,128)}, bf16[2,4,4,512,128]{4,3,2,1,0:T(8,128)(2,1)}, bf16[2,4,4,512,128]{4,3,2,1,0:T(8,128)(2,1)}, bf16[1024,2048]{1,0:T(8,128)(2,1)}) custom-call(bf16[1024,2048]{1,0:T(8,128)(2,1)} %bitcast.124, bf16[2048,768]{1,0:T(8,128)(2,1)} %bitcast.135, f32[1,128]{1,0:T(1,128)} %bitcast.122, ...), custom_call_target="tpu_custom_call" | custom-call | flops 35000000512 | bytes 105000000 | tf_op jit(solution)/shard_map/links_1/pallas_call | solution.py:117
  107.7 6.9 %all-to-all-start = ((bf16[128,8,2048]{2,1,0:T(8,128)(2,1)}), bf16[128,8,2048]{2,1,0:T(8,128)(2,1)}, u32[]{:S(2)}, u32[]{:S(2)}) async-start(bf16[128,8,2048]{2,1,0:T(8,128)(2,1)} %bitcast.99), calls=%async_computation | async-start | bytes 8388608 | tf_op jit(solution)/shard_map/all_to_all | solution.py:1350
  116.7 18.5 %attend.1 = (bf16[1024,512]{1,0:T(8,128)(2,1)}, bf16[1024,512]{1,0:T(8,128)(2,1)}, f32[4,1,1024]{2,1,0:T(1,128)}) custom-call(s32[4]{0:T(128)} %get-tuple-element.128.lo_ref, s32[4]{0:T(128)} %get-tuple-element.127.full_ref, s32[4]{0:T(128)} %copy-done.7, s32[64]{0:T(128)} %select_reduce_fusion.1.slot_ref, f32[1024,512]{1,0:T(8,128)} %get-tuple-element.71.raw_ref, ...), custom_call_target="tpu_custom_call" | custom-call | flops 30000001024 | bytes 90000000 | tf_op jit(solution)/shard_map/attend/pallas_call | solution.py:1279
  135.2 50.3 %links_2.1 = (f32[128,2048]{1,0:T(8,128)}, bf16[128,2048]{1,0:T(8,128)(2,1)}, f32[128,128]{1,0:T(8,128)}, bf16[1024,2176]{1,0:T(8,128)(2,1)}) custom-call(bf16[1024,512]{1,0:T(8,128)(2,1)} %get-tuple-element.75.refs_0_.o_ref.refs_5_, bf16[2048,640]{1,0:T(8,128)(2,1)} %all-gather.2.cloned.1.call-done.refs_1_.w_ref, bf16[128,2048]{1,0:T(8,128)(2,1)} %refs_17_.1, ...), custom_call_target="tpu_custom_call" | custom-call | flops 30000001024 | bytes 90000000 | tf_op jit(solution)/shard_map/links_2/pallas_call | solution.py:117
  185.6 9.5 %all-to-all-start.1 = ((bf16[128,8,2176]{2,1,0:T(8,128)(2,1)}), bf16[128,8,2176]{2,1,0:T(8,128)(2,1)}, u32[]{:S(2)}, u32[]{:S(2)}) async-start(bf16[128,8,2176]{2,1,0:T(8,128)(2,1)} %bitcast.97), calls=%async_computation.1 | async-start | bytes 8912896 | tf_op jit(solution)/shard_map/all_to_all | solution.py:1350
  195.1 7.3 %fusion.2.plain_ref = f32[1024,768]{1,0:T(8,128)} fusion(bf16[1024,2048]{1,0:T(8,128)(2,1)} %bitcast.17, bf16[1,768,2048]{2,1,0:T(8,128)(2,1)S(1)} %copy-done), kind=kOutput, calls=%fused_computation.5 | convolution fusion | flops 3221225472 | bytes 10485760 | tf_op jit(solution)/shard_map/dot_general | solution.py:1018
  202.4 48.2 %all-to-all-done.1 = bf16[128,8,2176]{2,1,0:T(8,128)(2,1)} async-done(((bf16[128,8,2176]{2,1,0:T(8,128)(2,1)}), bf16[128,8,2176]{2,1,0:T(8,128)(2,1)}, u32[]{:S(2)}, u32[]{:S(2)}) %all-to-all-start.1) | async-done | bytes 4456480 | tf_op jit(solution)/shard_map/all_to_all | solution.py:1350
  250.6 19.2 %expert.1 = (bf16[1024,2176]{1,0:T(8,128)(2,1)}, bf16[1024,768]{1,0:T(8,128)(2,1)}, bf16[1024,768]{1,0:T(8,128)(2,1)}, bf16[1024,1536]{1,0:T(8,128)(2,1)}) custom-call(bf16[1024,2176]{1,0:T(8,128)(2,1)} %bitcast.19.rows_ref, f32[1024,768]{1,0:T(8,128)} %fusion.2.plain_ref, bf16[2048,1536]{1,0:T(8,128)(2,1)} %bitcast.117), custom_call_target="tpu_custom_call" | custom-call | flops 20000000000 | bytes 60000000 | tf_op jit(solution)/shard_map/expert/pallas_call | solution.py:1262
  269.8 11.6 %all-to-all-start.2 = ((bf16[128,8,2176]{2,1,0:T(8,128)(2,1)}), bf16[128,8,2176]{2,1,0:T(8,128)(2,1)}, u32[]{:S(2)}, u32[]{:S(2)}) async-start(bf16[128,8,2176]{2,1,0:T(8,128)(2,1)} %bitcast.96), calls=%async_computation.2 | async-start | bytes 8912896 | tf_op jit(solution)/shard_map/all_to_all | solution.py:1350
  282.3 6.5 %convolution_convert_fusion = bf16[1024,2048]{1,0:T(8,128)(2,1)} fusion(bf16[1024,768]{1,0:T(8,128)(2,1)} %get-tuple-element.86, bf16[1,768,2048]{2,1,0:T(8,128)(2,1)S(1)} %copy-done), kind=kOutput, calls=%fused_computation.3 | convolution fusion | flops 3223322624 | bytes 8912896 | tf_op jit(solution)/shard_map/dot_general | solution.py:1014
  288.9 7.7 %convolution_bitcast_fusion.1 = f32[1,768,2048]{2,1,0:T(8,128)} fusion(bf16[1024,768]{1,0:T(8,128)(2,1)S(1)} %copy-done.2, bf16[1024,2048]{1,0:T(8,128)(2,1)} %bitcast.17), kind=kOutput, calls=%fused_computation.2 | convolution fusion | flops 3221225472 | bytes 12058624 | tf_op jit(solution)/shard_map/dot_general | solution.py:1022
  296.6 11.4 %convolution_bitcast_fusion = f32[1,2048,1536]{2,1,0:T(8,128)} fusion(bf16[1024,1536]{1,0:T(8,128)(2,1)S(1)} %copy-done.8, bf16[1024,2176]{1,0:T(8,128)(2,1)} %bitcast.19.rows_ref), kind=kOutput, calls=%fused_computation | convolution fusion | flops 6442450944 | bytes 19922944 | tf_op jit(solution)/shard_map/dot_general | solution.py:1022
  307.9 29.0 %all-to-all-done.2 = bf16[128,8,2176]{2,1,0:T(8,128)(2,1)} async-done(((bf16[128,8,2176]{2,1,0:T(8,128)(2,1)}), bf16[128,8,2176]{2,1,0:T(8,128)(2,1)}, u32[]{:S(2)}, u32[]{:S(2)}) %all-to-all-start.2) | async-done | bytes 4456480 | tf_op jit(solution)/shard_map/all_to_all | solution.py:1350
  336.9 28.1 %links_3.1 = (f32[128,2048]{1,0:T(8,128)}, f32[1,2048]{1,0:T(1,128)}, bf16[2048,128]{1,0:T(8,128)(2,1)}, bf16[2,4,128,2048]{3,2,1,0:T(8,128)(2,1)}) custom-call(bf16[1024,2176]{1,0:T(8,128)(2,1)} %bitcast.23.refs_0_, bf16[2048,640]{1,0:T(8,128)(2,1)} %all-gather.2.cloned.1.call-done.refs_1_.w_ref, ...), custom_call_target="tpu_custom_call" | custom-call | flops 24999999488 | bytes 75000000 | tf_op jit(solution)/shard_map/links_3/pallas_call | solution.py:117
  365.1 11.6 %all-to-all-start.3 = ((bf16[128,8,2048]{2,1,0:T(8,128)(2,1)}), bf16[128,8,2048]{2,1,0:T(8,128)(2,1)}, u32[]{:S(2)}, u32[]{:S(2)}) async-start(bf16[128,8,2048]{2,1,0:T(8,128)(2,1)} %bitcast.98), calls=%async_computation.3 | async-start | bytes 8388608 | tf_op jit(solution)/shard_map/all_to_all | solution.py:1350
  376.7 36.7 %attend_back.1 = (bf16[1024,512]{1,0:T(8,128)(2,1)}, f32[1,128]{1,0:T(1,128)}, bf16[64,256,128]{2,1,0:T(8,128)(2,1)}, bf16[64,256,128]{2,1,0:T(8,128)(2,1)}) custom-call(s32[4]{0:T(128)} %get-tuple-element.128.lo_ref, s32[4]{0:T(128)} %get-tuple-element.127.full_ref, s32[4]{0:T(128)} %copy-done.7, s32[64]{0:T(128)} %select_reduce_fusion.1.slot_ref, ...), custom_call_target="tpu_custom_call" | custom-call | flops 40000000000 | bytes 120000000 | tf_op jit(solution)/shard_map/attend_back/pallas_call | solution.py:1308
  414.1 49.3 %links_4.1 = (bf16[512,128]{1,0:T(8,128)(2,1)}, bf16[512,128]{1,0:T(8,128)(2,1)}, bf16[2048,512]{1,0:T(8,128)(2,1)}, bf16[2048,512]{1,0:T(8,128)(2,1)}) custom-call(bf16[2,4,4,512,128]{4,3,2,1,0:T(8,128)(2,1)} %bitcast.133, bf16[2,4,4,512,128]{4,3,2,1,0:T(8,128)(2,1)} %bitcast.134, bf16[1024,2048]{1,0:T(8,128)(2,1)} %bitcast.125, ...), custom_call_target="tpu_custom_call" | custom-call | flops 35000000512 | bytes 105000000 | tf_op jit(solution)/shard_map/links_4/pallas_call | solution.py:117
  463.4 62.8 %links_5.1 = (bf16[4,32,512]{2,1,0:T(8,128)(2,1)}, bf16[4,32,512]{2,1,0:T(8,128)(2,1)}, f32[40,128]{1,0:T(8,128)}, bf16[4,32,256]{2,1,0:T(8,128)(2,1)}, bf16[8,3...) custom-call(bf16[512,128]{1,0:T(8,128)(2,1)} %get-tuple-element.100.refs_0_, ...), custom_call_target="tpu_custom_call" | custom-call | flops 49999998976 | bytes 150000000 | tf_op jit(solution)/shard_map/links_5/pallas_call | solution.py:117
  526.2 1.3 slice_bitcast_fusion
  527.5 1.3 slice_bitcast_fusion.2
  528.8 0.9 convert_bitcast_fusion.1
  530.4 0.9 reshape.322
  532.7 0.9 convert_bitcast_fusion
  534.4 0.9 convert_reduce_fusion
  535.9 1.9 copy.73
  537.8 2.3 copy.74
  (65 shorter events, 13.4 us)
Async XLA Ops:
  7.2 187.9 %copy-start = (bf16[1,768,2048]{2,1,0:T(8,128)(2,1)S(1)}, bf16[1,768,2048]{2,1,0:T(8,128)(2,1)}, u32[]{:S(2)}) copy-start(bf16[1,768,2048]{2,1,0:T(8,128)(2,1)} %param.28) | copy-start | bytes 9437188
  7.2 128.0 %all-gather.2.cloned.1.call-start = ((), (), s32[]{:S(2)}) async-start(), calls=%async_computation.4 | async-start | bytes 2785280 | tf_op jit(solution)/shard_map/all_gather | solution.py:1422
  9.0 58.0 %copy-start.7 = (s32[4]{0:T(128)}, s32[4]{0:T(128)S(1)}, u32[]{:S(2)}) copy-start(s32[4]{0:T(128)S(1)} %select_reduce_fusion.2.last_ref) | copy-start | bytes 52
  107.7 7.9 %copy-start.6 = (s32[64]{0:T(128)S(1)}, s32[64]{0:T(128)}, u32[]{:S(2)}) copy-start(s32[64]{0:T(128)} %param.30) | copy-start | bytes 772
  107.7 77.9 %all-to-all-start = ((bf16[128,8,2048]{2,1,0:T(8,128)(2,1)}), bf16[128,8,2048]{2,1,0:T(8,128)(2,1)}, u32[]{:S(2)}, u32[]{:S(2)}) async-start(bf16[128,8,2048]{2,1,0:T(8,128)(2,1)} %bitcast.99), calls=%async_computation | async-start | bytes 8388608 | tf_op jit(solution)/shard_map/all_to_all | solution.py:1350
  185.6 65.0 %all-to-all-start.1 = ((bf16[128,8,2176]{2,1,0:T(8,128)(2,1)}), bf16[128,8,2176]{2,1,0:T(8,128)(2,1)}, u32[]{:S(2)}, u32[]{:S(2)}) async-start(bf16[128,8,2176]{2,1,0:T(8,128)(2,1)} %bitcast.97), calls=%async_computation.1 | async-start | bytes 8912896 | tf_op jit(solution)/shard_map/all_to_all | solution.py:1350
  269.8 67.1 %all-to-all-start.2 = ((bf16[128,8,2176]{2,1,0:T(8,128)(2,1)}), bf16[128,8,2176]{2,1,0:T(8,128)(2,1)}, u32[]{:S(2)}, u32[]{:S(2)}) async-start(bf16[128,8,2176]{2,1,0:T(8,128)(2,1)} %bitcast.96), calls=%async_computation.2 | async-start | bytes 8912896 | tf_op jit(solution)/shard_map/all_to_all | solution.py:1350
  282.3 6.5 %copy-start.2 = (bf16[1024,768]{1,0:T(8,128)(2,1)S(1)}, bf16[1024,768]{1,0:T(8,128)(2,1)}, u32[]{:S(2)}) copy-start(bf16[1024,768]{1,0:T(8,128)(2,1)} %get-tuple-element.118) | copy-start | bytes 4718596
  288.9 7.7 %copy-start.8 = (bf16[1024,1536]{1,0:T(8,128)(2,1)S(1)}, bf16[1024,1536]{1,0:T(8,128)(2,1)}, u32[]{:S(2)}) copy-start(bf16[1024,1536]{1,0:T(8,128)(2,1)} %get-tuple-element.117) | copy-start | bytes 9437188
  365.1 98.4 %all-to-all-start.3 = ((bf16[128,8,2048]{2,1,0:T(8,128)(2,1)}), bf16[128,8,2048]{2,1,0:T(8,128)(2,1)}, u32[]{:S(2)}, u32[]{:S(2)}) async-start(bf16[128,8,2048]{2,1,0:T(8,128)(2,1)} %bitcast.98), calls=%async_computation.3 | async-start | bytes 8388608 | tf_op jit(solution)/shard_map/all_to_all | solution.py:1350
  376.7 36.7 %copy-start.4 = (f32[1,2048]{1,0:T(1,128)S(1)}, f32[1,2048]{1,0:T(1,128)}, u32[]{:S(2)}) copy-start(f32[1,2048]{1,0:T(1,128)} %get-tuple-element.105) | copy-start | bytes 24580
  376.7 37.4 %copy-start.3 = (f32[2048]{0:T(1024)S(1)}, f32[2048]{0:T(1024)}, u32[]{:S(2)}) copy-start(f32[2048]{0:T(1024)} %param.18) | copy-start | bytes 24580
  414.1 49.3 %copy-start.5 = (f32[10240]{0:T(1024)}, f32[10240]{0:T(1024)S(1)}, u32[]{:S(2)}) copy-start(f32[10240]{0:T(1024)S(1)} %constant_dynamic-update-slice_fusion) | copy-start | bytes 122884
  463.4 76.7 %copy-start.1 = (bf16[1,768,2048]{2,1,0:T(8,128)(2,1)S(1)}, bf16[1,768,2048]{2,1,0:T(8,128)(2,1)}, u32[]{:S(2)}) copy-start(bf16[1,768,2048]{2,1,0:T(8,128)(2,1)} %param.28) | copy-start | bytes 9437188
Sparse Core Ops, SparseCore 0:
  69.6 45.4 all-gather.1

commit v3 on v2

--- a/solution.py
+++ b/solution.py
@@ -280,10 +280,10 @@
     )
 
 
-def plane_gather_flow(arrays, first, second, ahead=None):
+def plane_gather_flow(arrays, first, second, ahead=None, beside=None):
     to_core = ahead is None
     if ahead == "zhc":
-        shard = (4, arrays[0][0].shape[0], sum(columns for _, columns, _ in arrays))
+        shard = (4, arrays[0][0].shape[0], sum(columns for _, columns, _ in arrays) + (beside.shape[-1] if beside else 0))
     elif ahead == "z":
         shard = (8,) + arrays[0][0].shape
     else:
@@ -329,6 +329,11 @@
             yield Clock.now + HOP + 7.0
             for copy in early:
                 copy.wait()
+            if beside:
+                yield beside
+                for g in range(4):
+                    pair = beside.ref[2 * g].astype(F32) + beside.ref[2 * g + 1].astype(F32)
+                    stage[g, :, shard[2] - beside.shape[-1] :] = pair.astype(BF)
             src = stage
         else:
             src = arrays.ref
@@ -401,36 +406,26 @@
     )
 
 
-def ring_exchange_flow(array, columns, kind):
-    n, rows = SIZES[kind], array.shape[0]
-
+def stack_flow(array, made):
     def steps(ins, outs, scratch):
-        (src,), (out,) = ins, outs
-        send, recv, local = scratch
-        mine, at = peers_of(kind)
-
-        def part(to):
-            return src if kind == "z" else src.at[:, pl.ds(pl.multiple_of(to * columns, columns), columns)]
-
-        own = pltpu.make_async_copy(part(mine), out.at[mine], local.at[0])
+        (src,) = ins
+        stage, send, recv, local = scratch
+        mine, at = peers_of("z")
+        own = pltpu.make_async_copy(src, stage.at[mine], local.at[0])
         own.start()
         yield
         copies = []
-        for k in range(1, n):
-            to = lax.rem(mine + k, n)
-            copies.append(remote(part(to), out.at[mine], send.at[k], recv.at[k], at(to)))
+        for k in range(1, 8):
+            copies.append(remote(src, stage.at[mine], send.at[k], recv.at[k], at(lax.rem(mine + k, 8))))
             copies[-1].start()
-        yield 40.0
+        yield Clock.now + HOP + 6.0
         own.wait()
         for copy in copies:
             copy.wait()
+        made.ref = stage
 
     return Flow(
-        [(array, pl.ANY)],
-        [((n, rows, columns), BF, pltpu.VMEM)],
-        [dma(n), dma(n), dma(1)],
-        [(kind, k) for k in range(1, n)],
-        steps,
+        [(array, pl.ANY)], [], [pltpu.VMEM((8,) + array.shape, BF), dma(8), dma(8), dma(1)], [("z", k) for k in range(1, 8)], steps
     )
 
 
@@ -1402,12 +1397,13 @@
     out_pack = w_out.reshape(4, q_cols, depth).transpose(2, 0, 1).reshape(depth, -1)
     side = lax.axis_index("head") == jnp.arange(2, dtype=jnp.int32)
     router_pack = jnp.where(side[None, :, None], w_router.T[:, None, :], 0).astype(BF).reshape(depth, experts)
-    w_qkv, out_part, router_part, group_tokens, assign_low, chosen, cosine, sine = launch(
+    stacked_router = Made(8, depth, experts)
+    w_qkv, w_rest, group_tokens, assign_low, chosen, cosine, sine = launch(
         [
             norm_flow(tokens, norm_gain[None], normed),
             plane_gather_flow([(w_query, q_cols, 1), (key_weight, size, 2), (value_weight, size, 2)], "x", "y", ahead="zhc"),
-            ring_exchange_flow(out_pack, q_cols, "zhc"),
-            ring_exchange_flow(router_pack, experts, "z"),
+            stack_flow(router_pack, stacked_router),
+            plane_gather_flow([(out_pack, q_cols, 1)], "y", "x", ahead="zhc", beside=stacked_router),
             ring_gather_flow(normed),
             tables_flow(routes, offsets, spacing, experts, cap),
         ],
@@ -1416,10 +1412,7 @@
     )
     normed_group = group_tokens.reshape(group_rows, width)
     w_qkv = w_qkv.reshape(width, -1)
-    router_part = jnp.sum(router_part.reshape(4, 2, depth, experts), axis=1)
-    w_rest = jnp.concatenate([out_part, router_part], axis=2).reshape(4 * depth, -1)
-    planes = [[j * 4 + r for j in range(16)] for r in range(4)]
-    w_rest = lax.all_gather(w_rest, "blk", axis_index_groups=planes, axis=0, tiled=True)
+    w_rest = w_rest.reshape(width, -1)
 
     q_gain, k_gain = query_gain[None], key_gain[None]
     key, value = Made(group_rows // 2, size), Made(group_rows // 2, size)

time: 554 us -> 536 us (0.968)
  between operations: 14.8 us -> 1.43 us
    pallas_call x1, Pallas kernels: 36.7 us -> 29.3 us  [attend_backward(): pl.pallas_call(attend_backward_kernel, out_shape=outs, grid_spec=pltpu.Pr...]
  transfers between devices with their start and end apart: 5 -> 4, of which waited for: 2 -> 2; matrix products, arithmetic and copies ran while one was open for 7% -> 7% of each run, Pallas kernels for 35% -> 28%
where the time goes in v3:
time: 536 us; the launch traced here: 526 us
  Pallas kernels  348 us (65%)
  waiting for transfers between devices  77.2 us (14%)
  starting transfers between devices  39.5 us (7%)
  matrix products  32.9 us (6%)
  local copies, waits for them, and re-layouts  18.2 us (3%)
  other arithmetic  8.82 us (2%)
    pallas_call x6, Pallas kernels, launch(): pl.pallas_call(kernel, out_shape=tuple((jax.ShapeDtypeStruct(s, d) for f...  283 us
    all_to_all x4, waiting for transfers between devices, all_to_all(): lax.all_to_all(stacked, ('head', 'blk'), split_axis=0, concat_axis=0, til...  77.2 us
    all_to_all x4, starting transfers between devices, all_to_all(): lax.all_to_all(stacked, ('head', 'blk'), split_axis=0, concat_axis=0, til...  39.5 us
    pallas_call x1, Pallas kernels, attend_backward(): pl.pallas_call(attend_backward_kernel, out_shape=outs, grid_spec=pltpu.Pr...  29.3 us
    pallas_call x1, Pallas kernels, expert(): pl.pallas_call(expert_kernel, out_shape=outs, grid=(count // block,), in_...  19.2 us
    dot_general x2, matrix products, dot_tn(): lax.dot_general(a, b, (((0,), (0,)), ((), ())), preferred_element_type=F32)  19 us
    pallas_call x1, Pallas kernels, attend_forward(): pl.pallas_call(attend_forward_kernel, out_shape=outs, grid_spec=pltpu.Pre...  16.4 us
  transfers between devices with their start and end apart: 4, of which 2 were waited for; matrix products, arithmetic and copies ran while one was open for 7% of the time, Pallas kernels for 28%

profile of v3, /device:TPU:1, one launch (start us, length us, event | category | flops | bytes accessed | tf_op | source)
XLA Modules:
  0.0 525.7 jit_solution(7827683069166053026)
XLA Ops:
  0.7 0.8 broadcast_add_fusion
  1.5 0.9 select_reduce_fusion.2.last_ref
  4.4 1.0 reshape.285
  6.1 1.4 copy.52.refs_7_
  7.5 0.7 select_reduce_fusion
  10.1 52.5 %links_0.1 = (bf16[4,4,4,32,768]{4,3,2,1,0:T(8,128)(2,1)}, bf16[4,4,4,32,640]{4,3,2,1,0:T(8,128)(2,1)}, bf16[2,4,128,2048]{3,2,1,0:T(8,128)(2,1)}, bf16[128,1024...) custom-call(bf16[128,2048]{1,0:T(8,128)(2,1)} %refs_17_.1, ...), custom_call_target="tpu_custom_call" | custom-call | flops 44999999488 | bytes 135000000 | tf_op jit(solution)/shard_map/links_0/pallas_call | solution.py:117
  62.6 36.1 %links_1.1 = (f32[1024,512]{1,0:T(8,128)}, f32[512,128]{1,0:T(8,128)}, bf16[2,4,4,512,128]{4,3,2,1,0:T(8,128)(2,1)}, bf16[2,4,4,512,128]{4,3,2,1,0:T(8,128)(2,1)}, bf16[1024,2048]{1,0:T(8,128)(2,1)}) custom-call(bf16[1024,2048]{1,0:T(8,128)(2,1)} %bitcast.121, bf16[2048,768]{1,0:T(8,128)(2,1)} %bitcast.132, f32[1,128]{1,0:T(1,128)} %bitcast.119, ...), custom_call_target="tpu_custom_call" | custom-call | flops 35000000512 | bytes 105000000 | tf_op jit(solution)/shard_map/links_1/pallas_call | solution.py:117
  98.7 6.8 %all-to-all-start = ((bf16[128,8,2048]{2,1,0:T(8,128)(2,1)}), bf16[128,8,2048]{2,1,0:T(8,128)(2,1)}, u32[]{:S(2)}, u32[]{:S(2)}) async-start(bf16[128,8,2048]{2,1,0:T(8,128)(2,1)} %bitcast.97), calls=%async_computation | async-start | bytes 8388608 | tf_op jit(solution)/shard_map/all_to_all | solution.py:1345
  107.7 16.4 %attend.1 = (bf16[1024,512]{1,0:T(8,128)(2,1)}, bf16[1024,512]{1,0:T(8,128)(2,1)}, f32[4,1,1024]{2,1,0:T(1,128)}) custom-call(s32[4]{0:T(128)} %get-tuple-element.126.lo_ref, s32[4]{0:T(128)} %get-tuple-element.125.full_ref, s32[4]{0:T(128)} %copy-done.7, s32[64]{0:T(128)} %select_reduce_fusion.1.slot_ref, f32[1024,512]{1,0:T(8,128)} %get-tuple-element.70.raw_ref, ...), custom_call_target="tpu_custom_call" | custom-call | flops 30000001024 | bytes 90000000 | tf_op jit(solution)/shard_map/attend/pallas_call | solution.py:1274
  124.1 52.5 %links_2.1 = (f32[128,2048]{1,0:T(8,128)}, bf16[128,2048]{1,0:T(8,128)(2,1)}, f32[128,128]{1,0:T(8,128)}, bf16[1024,2176]{1,0:T(8,128)(2,1)}) custom-call(bf16[1024,512]{1,0:T(8,128)(2,1)} %get-tuple-element.74.refs_0_.o_ref.refs_5_, bf16[2048,640]{1,0:T(8,128)(2,1)} %bitcast.134, bf16[128,2048]{1,0:T(8,128)(2,1)} %refs_17_.1, f32[1,2048]{1,0:T(1,128)} %bitcast.115, ...), custom_call_target="tpu_custom_call" | custom-call | flops 30000001024 | bytes 90000000 | tf_op jit(solution)/shard_map/links_2/pallas_call | solution.py:117
  176.6 9.5 %all-to-all-start.1 = ((bf16[128,8,2176]{2,1,0:T(8,128)(2,1)}), bf16[128,8,2176]{2,1,0:T(8,128)(2,1)}, u32[]{:S(2)}, u32[]{:S(2)}) async-start(bf16[128,8,2176]{2,1,0:T(8,128)(2,1)} %bitcast.95), calls=%async_computation.1 | async-start | bytes 8912896 | tf_op jit(solution)/shard_map/all_to_all | solution.py:1345
  186.1 7.3 %fusion.2.plain_ref = f32[1024,768]{1,0:T(8,128)} fusion(bf16[1024,2048]{1,0:T(8,128)(2,1)} %bitcast.16, bf16[1,768,2048]{2,1,0:T(8,128)(2,1)S(1)} %copy-done), kind=kOutput, calls=%fused_computation.5 | convolution fusion | flops 3221225472 | bytes 10485760 | tf_op jit(solution)/shard_map/dot_general | solution.py:1013
  193.4 48.2 %all-to-all-done.1 = bf16[128,8,2176]{2,1,0:T(8,128)(2,1)} async-done(((bf16[128,8,2176]{2,1,0:T(8,128)(2,1)}), bf16[128,8,2176]{2,1,0:T(8,128)(2,1)}, u32[]{:S(2)}, u32[]{:S(2)}) %all-to-all-start.1) | async-done | bytes 4456480 | tf_op jit(solution)/shard_map/all_to_all | solution.py:1345
  241.6 19.2 %expert.1 = (bf16[1024,2176]{1,0:T(8,128)(2,1)}, bf16[1024,768]{1,0:T(8,128)(2,1)}, bf16[1024,768]{1,0:T(8,128)(2,1)}, bf16[1024,1536]{1,0:T(8,128)(2,1)}) custom-call(bf16[1024,2176]{1,0:T(8,128)(2,1)} %bitcast.18.rows_ref, f32[1024,768]{1,0:T(8,128)} %fusion.2.plain_ref, bf16[2048,1536]{1,0:T(8,128)(2,1)} %bitcast.114), custom_call_target="tpu_custom_call" | custom-call | flops 20000000000 | bytes 60000000 | tf_op jit(solution)/shard_map/expert/pallas_call | solution.py:1257
  260.8 11.6 %all-to-all-start.2 = ((bf16[128,8,2176]{2,1,0:T(8,128)(2,1)}), bf16[128,8,2176]{2,1,0:T(8,128)(2,1)}, u32[]{:S(2)}, u32[]{:S(2)}) async-start(bf16[128,8,2176]{2,1,0:T(8,128)(2,1)} %bitcast.94), calls=%async_computation.2 | async-start | bytes 8912896 | tf_op jit(solution)/shard_map/all_to_all | solution.py:1345
  273.3 6.5 %convolution_convert_fusion = bf16[1024,2048]{1,0:T(8,128)(2,1)} fusion(bf16[1024,768]{1,0:T(8,128)(2,1)} %get-tuple-element.84, bf16[1,768,2048]{2,1,0:T(8,128)(2,1)S(1)} %copy-done), kind=kOutput, calls=%fused_computation.3 | convolution fusion | flops 3223322624 | bytes 8912896 | tf_op jit(solution)/shard_map/dot_general | solution.py:1009
  279.9 7.7 %convolution_bitcast_fusion.1 = f32[1,768,2048]{2,1,0:T(8,128)} fusion(bf16[1024,768]{1,0:T(8,128)(2,1)S(1)} %copy-done.2, bf16[1024,2048]{1,0:T(8,128)(2,1)} %bitcast.16), kind=kOutput, calls=%fused_computation.2 | convolution fusion | flops 3221225472 | bytes 12058624 | tf_op jit(solution)/shard_map/dot_general | solution.py:1017
  287.6 11.4 %convolution_bitcast_fusion = f32[1,2048,1536]{2,1,0:T(8,128)} fusion(bf16[1024,1536]{1,0:T(8,128)(2,1)S(1)} %copy-done.8, bf16[1024,2176]{1,0:T(8,128)(2,1)} %bitcast.18.rows_ref), kind=kOutput, calls=%fused_computation | convolution fusion | flops 6442450944 | bytes 19922944 | tf_op jit(solution)/shard_map/dot_general | solution.py:1017
  298.9 29.0 %all-to-all-done.2 = bf16[128,8,2176]{2,1,0:T(8,128)(2,1)} async-done(((bf16[128,8,2176]{2,1,0:T(8,128)(2,1)}), bf16[128,8,2176]{2,1,0:T(8,128)(2,1)}, u32[]{:S(2)}, u32[]{:S(2)}) %all-to-all-start.2) | async-done | bytes 4456480 | tf_op jit(solution)/shard_map/all_to_all | solution.py:1345
  327.9 28.1 %links_3.1 = (f32[128,2048]{1,0:T(8,128)}, f32[1,2048]{1,0:T(1,128)}, bf16[2048,128]{1,0:T(8,128)(2,1)}, bf16[2,4,128,2048]{3,2,1,0:T(8,128)(2,1)}) custom-call(bf16[1024,2176]{1,0:T(8,128)(2,1)} %bitcast.22.refs_0_, bf16[2048,640]{1,0:T(8,128)(2,1)} %bitcast.135, bf16[128,1024]{1,0:T(8,128)(2,1)} %get-tuple-element.69.refs_5_.refs_2_.refs_15_, ...), custom_call_target="tpu_custom_call" | custom-call | flops 24999999488 | bytes 75000000 | tf_op jit(solution)/shard_map/links_3/pallas_call | solution.py:117
  356.1 11.6 %all-to-all-start.3 = ((bf16[128,8,2048]{2,1,0:T(8,128)(2,1)}), bf16[128,8,2048]{2,1,0:T(8,128)(2,1)}, u32[]{:S(2)}, u32[]{:S(2)}) async-start(bf16[128,8,2048]{2,1,0:T(8,128)(2,1)} %bitcast.96), calls=%async_computation.3 | async-start | bytes 8388608 | tf_op jit(solution)/shard_map/all_to_all | solution.py:1345
  367.7 29.3 %attend_back.1 = (bf16[1024,512]{1,0:T(8,128)(2,1)}, f32[1,128]{1,0:T(1,128)}, bf16[64,256,128]{2,1,0:T(8,128)(2,1)}, bf16[64,256,128]{2,1,0:T(8,128)(2,1)}) custom-call(s32[4]{0:T(128)} %get-tuple-element.126.lo_ref, s32[4]{0:T(128)} %get-tuple-element.125.full_ref, s32[4]{0:T(128)} %copy-done.7, s32[64]{0:T(128)} %select_reduce_fusion.1.slot_ref, ...), custom_call_target="tpu_custom_call" | custom-call | flops 40000000000 | bytes 120000000 | tf_op jit(solution)/shard_map/attend_back/pallas_call | solution.py:1303
  397.8 51.1 %links_4.1 = (bf16[512,128]{1,0:T(8,128)(2,1)}, bf16[512,128]{1,0:T(8,128)(2,1)}, bf16[2048,512]{1,0:T(8,128)(2,1)}, bf16[2048,512]{1,0:T(8,128)(2,1)}) custom-call(bf16[2,4,4,512,128]{4,3,2,1,0:T(8,128)(2,1)} %bitcast.130, bf16[2,4,4,512,128]{4,3,2,1,0:T(8,128)(2,1)} %bitcast.131, bf16[1024,2048]{1,0:T(8,128)(2,1)} %bitcast.122, ...), custom_call_target="tpu_custom_call" | custom-call | flops 35000000512 | bytes 105000000 | tf_op jit(solution)/shard_map/links_4/pallas_call | solution.py:117
  448.9 62.5 %links_5.1 = (bf16[4,32,512]{2,1,0:T(8,128)(2,1)}, bf16[4,32,512]{2,1,0:T(8,128)(2,1)}, f32[40,128]{1,0:T(8,128)}, bf16[4,32,256]{2,1,0:T(8,128)(2,1)}, bf16[8,3...) custom-call(bf16[512,128]{1,0:T(8,128)(2,1)} %get-tuple-element.98.refs_0_, ...), custom_call_target="tpu_custom_call" | custom-call | flops 49999998976 | bytes 150000000 | tf_op jit(solution)/shard_map/links_5/pallas_call | solution.py:117
  511.4 1.3 slice_bitcast_fusion
  512.7 1.3 slice_bitcast_fusion.2
  514.0 0.9 convert_bitcast_fusion.1
  515.6 0.9 reshape.318
  517.9 0.9 convert_bitcast_fusion
  519.6 0.9 convert_reduce_fusion
  521.1 1.9 copy.73
  523.0 2.3 copy.74
  (60 shorter events, 11.8 us)
Async XLA Ops:
  0.6 185.4 %copy-start = (bf16[1,768,2048]{2,1,0:T(8,128)(2,1)S(1)}, bf16[1,768,2048]{2,1,0:T(8,128)(2,1)}, u32[]{:S(2)}) copy-start(bf16[1,768,2048]{2,1,0:T(8,128)(2,1)} %param.28) | copy-start | bytes 9437188
  2.4 60.1 %copy-start.7 = (s32[4]{0:T(128)}, s32[4]{0:T(128)S(1)}, u32[]{:S(2)}) copy-start(s32[4]{0:T(128)S(1)} %select_reduce_fusion.2.last_ref) | copy-start | bytes 52
  98.7 7.2 %copy-start.6 = (s32[64]{0:T(128)S(1)}, s32[64]{0:T(128)}, u32[]{:S(2)}) copy-start(s32[64]{0:T(128)} %param.30) | copy-start | bytes 772
  98.7 77.8 %all-to-all-start = ((bf16[128,8,2048]{2,1,0:T(8,128)(2,1)}), bf16[128,8,2048]{2,1,0:T(8,128)(2,1)}, u32[]{:S(2)}, u32[]{:S(2)}) async-start(bf16[128,8,2048]{2,1,0:T(8,128)(2,1)} %bitcast.97), calls=%async_computation | async-start | bytes 8388608 | tf_op jit(solution)/shard_map/all_to_all | solution.py:1345
  176.6 65.0 %all-to-all-start.1 = ((bf16[128,8,2176]{2,1,0:T(8,128)(2,1)}), bf16[128,8,2176]{2,1,0:T(8,128)(2,1)}, u32[]{:S(2)}, u32[]{:S(2)}) async-start(bf16[128,8,2176]{2,1,0:T(8,128)(2,1)} %bitcast.95), calls=%async_computation.1 | async-start | bytes 8912896 | tf_op jit(solution)/shard_map/all_to_all | solution.py:1345
  260.8 67.1 %all-to-all-start.2 = ((bf16[128,8,2176]{2,1,0:T(8,128)(2,1)}), bf16[128,8,2176]{2,1,0:T(8,128)(2,1)}, u32[]{:S(2)}, u32[]{:S(2)}) async-start(bf16[128,8,2176]{2,1,0:T(8,128)(2,1)} %bitcast.94), calls=%async_computation.2 | async-start | bytes 8912896 | tf_op jit(solution)/shard_map/all_to_all | solution.py:1345
  273.3 6.5 %copy-start.2 = (bf16[1024,768]{1,0:T(8,128)(2,1)S(1)}, bf16[1024,768]{1,0:T(8,128)(2,1)}, u32[]{:S(2)}) copy-start(bf16[1024,768]{1,0:T(8,128)(2,1)} %get-tuple-element.116) | copy-start | bytes 4718596
  279.9 7.7 %copy-start.8 = (bf16[1024,1536]{1,0:T(8,128)(2,1)S(1)}, bf16[1024,1536]{1,0:T(8,128)(2,1)}, u32[]{:S(2)}) copy-start(bf16[1024,1536]{1,0:T(8,128)(2,1)} %get-tuple-element.115) | copy-start | bytes 9437188
  356.1 92.8 %all-to-all-start.3 = ((bf16[128,8,2048]{2,1,0:T(8,128)(2,1)}), bf16[128,8,2048]{2,1,0:T(8,128)(2,1)}, u32[]{:S(2)}, u32[]{:S(2)}) async-start(bf16[128,8,2048]{2,1,0:T(8,128)(2,1)} %bitcast.96), calls=%async_computation.3 | async-start | bytes 8388608 | tf_op jit(solution)/shard_map/all_to_all | solution.py:1345
  367.7 29.4 %copy-start.4 = (f32[1,2048]{1,0:T(1,128)S(1)}, f32[1,2048]{1,0:T(1,128)}, u32[]{:S(2)}) copy-start(f32[1,2048]{1,0:T(1,128)} %get-tuple-element.103) | copy-start | bytes 24580
  367.7 30.0 %copy-start.3 = (f32[2048]{0:T(1024)S(1)}, f32[2048]{0:T(1024)}, u32[]{:S(2)}) copy-start(f32[2048]{0:T(1024)} %param.18) | copy-start | bytes 24580
  397.8 51.1 %copy-start.5 = (f32[10240]{0:T(1024)}, f32[10240]{0:T(1024)S(1)}, u32[]{:S(2)}) copy-start(f32[10240]{0:T(1024)S(1)} %constant_dynamic-update-slice_fusion) | copy-start | bytes 122884
  448.9 76.4 %copy-start.1 = (bf16[1,768,2048]{2,1,0:T(8,128)(2,1)S(1)}, bf16[1,768,2048]{2,1,0:T(8,128)(2,1)}, u32[]{:S(2)}) copy-start(bf16[1,768,2048]{2,1,0:T(8,128)(2,1)} %param.28) | copy-start | bytes 9437188
